TPU v7x, 128 devices: a whole 4x4x4 slice. The times are simulated.
128 devices in a mesh: rep: 8 (over z_lo, y), fsdp: 16 (over x, z_hi, core).
Axes of the slice: x: 4, y: 4, z: 4 (z_hi: 2, z_lo: 2; z = z_hi * 2 + z_lo), core: 2. Of those that a mesh axis runs over, the one named last changes fastest.
Arguments:
- attn_out: bfloat16 [65536, 2048], P(('rep', 'fsdp')), may hold values from -6 to 6
- grad_out: bfloat16 [65536, 4608], P(('rep', 'fsdp')), may hold values from -6 to 6
- inner_w: bfloat16 [8, 2048, 4608], P('rep', 'fsdp'), may hold values from -6 to 6
- anchor: float32 [2048, 4608], P('fsdp', 'rep'), may hold values from -6 to 6
- momentum: float32 [2048, 4608], P('fsdp', 'rep'), may hold values from -4 to 4
- delayed: float32 [2048, 4608], P('fsdp', 'rep'), may hold values from -4 to 4
Outputs:
- input_grad: bfloat16 [65536, 2048], P(('rep', 'fsdp'))
- new_inner: bfloat16 [8, 2048, 4608], P('rep', 'fsdp')
- new_anchor: float32 [2048, 4608], P('fsdp', 'rep')
- new_momentum: float32 [2048, 4608], P('fsdp', 'rep')
- outer_grad: float32 [2048, 4608], P('fsdp', 'rep')
All inputs are finite; a program needn't handle non-finite values.
Results may differ from a plain program's by a relative error of at most 0.015.
Values may be sent and summed in bfloat16 or wider, within the bound.
A program may use at most 256 MiB of HBM per device.

v0:
```python
import jax
import jax.numpy as jnp
from jax import lax
from jax.sharding import PartitionSpec as P


def advance(anchor, momentum, delayed):
    new_momentum = 0.9 * momentum + delayed
    new_anchor = anchor - 0.7 * (delayed + 0.9 * new_momentum)
    anchor_full = lax.all_gather(new_anchor.astype(jnp.bfloat16), "rep", axis=1, tiled=True).astype(
        new_anchor.dtype
    )
    return (new_momentum, new_anchor, anchor_full)


def per_device(attn_out, grad_out, inner_w, anchor, momentum, delayed):
    weights = inner_w[0]
    factor = grad_out.shape[1] ** (-0.5)
    early = None
    product_cols = lax.dot_general(
        grad_out,
        lax.all_gather(weights, "fsdp", axis=0, tiled=True),
        (((1,), (1,)), ((), ())),
        preferred_element_type=jnp.float32,
    )
    input_grad = (product_cols * factor).astype(jnp.bfloat16)
    product_rows = lax.dot_general(
        attn_out, grad_out, (((0,), (0,)), ((), ())), preferred_element_type=jnp.float32
    )
    weight_grad = lax.psum_scatter(
        (product_rows * factor).astype(jnp.bfloat16), "fsdp", scatter_dimension=0, tiled=True
    ).astype(jnp.float32)
    stepped = (weights.astype(jnp.float32) - weight_grad).astype(jnp.bfloat16)
    summed = lax.psum_scatter(
        stepped.astype(jnp.float32).astype(jnp.bfloat16), "rep", scatter_dimension=1, tiled=True
    ).astype(jnp.float32)
    outer_grad = anchor - summed / lax.axis_size("rep")
    early = advance(anchor, momentum, delayed)
    new_momentum, new_anchor, anchor_full = early
    merged = (0.5 * anchor_full + 0.5 * stepped.astype(jnp.float32)).astype(jnp.bfloat16)
    return (input_grad, merged[None], new_anchor, new_momentum, outer_grad)


def solution(mesh):
    return jax.shard_map(
        per_device,
        mesh=mesh,
        in_specs=(
            P(("rep", "fsdp"), None),
            P(("rep", "fsdp"), None),
            P("rep", "fsdp", None),
            P("fsdp", "rep"),
            P("fsdp", "rep"),
            P("fsdp", "rep"),
        ),
        out_specs=(
            P(("rep", "fsdp"), None),
            P("rep", "fsdp", None),
            P("fsdp", "rep"),
            P("fsdp", "rep"),
            P("fsdp", "rep"),
        ),
        check_vma=False,
    )
```

profile of v0, /device:TPU:1, one launch (start us, length us, event | category | flops | bytes accessed | tf_op | source)
XLA Modules:
  0.0 344.4 jit_solution(13462560101282021003)
XLA Ops:
  8.0 0.0 copy-start
  8.0 0.0 all-gather.4.cloned.1.call-start
  8.1 2.2 fusion.7
  10.3 0.0 all-gather.4.cloned.1.call-update
  10.3 0.0 reduce-scatter.5.cloned.1.call-start
  10.3 0.0 copy-done
  10.3 15.1 %multiply_convert_fusion = bf16[2048,4608]{1,0:T(8,128)(2,1)} fusion(bf16[512,2048]{1,0:T(8,128)(2,1)S(1)} %copy-done, bf16[512,4608]{1,0:T(8,128)(2,1)} %param.7), kind=kOutput, calls=%fused_computation | convolution fusion | flops 9682550784 | bytes 25690112 | tf_op jit(solution)/shard_map/dot_general | solution.py:27
  25.5 0.0 reduce-scatter.5.cloned.1.call-update
  25.5 0.0 copy-start.1
  25.5 0.0 reduce-scatter.7.cloned.1.call-start
  25.6 23.3 %all-gather.4.cloned.1.call-done = bf16[128,4608]{0,1:T(8,128)(2,1)} async-done(((bf16[128,576]{0,1:T(8,128)(2,1)}), bf16[128,4608]{0,1:T(8,128)(2,1)}) %all-gather.4.cloned.1.call-update) | async-done | bytes 1179664 | tf_op jit(solution)/shard_map/all_gather | solution.py:10
  48.9 2.5 copy.19
  51.4 134.2 %reduce-scatter.5.cloned.1.call-done = bf16[128,4608]{1,0:T(8,128)(2,1)} async-done(((bf16[2048,4608]{1,0:T(8,128)(2,1)}), bf16[128,4608]{1,0:T(8,128)(2,1)}) %reduce-scatter.5.cloned.1.call-update) | async-done | bytes 1179664 | tf_op jit(solution)/shard_map/reduce_scatter | solution.py:30
  185.5 0.0 copy-done.1
  185.5 3.6 %fusion.5 = (bf16[1,128,4608]{2,1,0:T(8,128)(2,1)}, bf16[128,4608]{1,0:T(8,128)(2,1)}) fusion(bf16[128,4608]{1,0:T(8,128)(2,1)} %copy.19, bf16[128,4608]{1,0:T(8,128)(2,1)} %reduce-scatter.5.cloned.1.call-done, bf16[1,128,4608]{2,1,0:T(8,128)(2,1)S(1)} %copy-done.1), kind=kLoop, calls=%fused_computation.7 | loop fusion | flops 5308416 | bytes 5898240 | tf_op jit(solution)/shard_map/broadcast_in_dim | solution.py:41
  189.1 0.0 copy-start.2
  189.1 2.4 copy.22
  191.5 0.0 reduce-scatter.7.cloned.1.call-update
  191.5 0.0 all-gather.6.cloned.1.call-start
  191.6 0.5 all-gather.6.cloned.1.call-update
  192.1 0.0 copy-done.2
  192.1 0.2 copy.20
  192.3 32.4 %reduce-scatter.7.cloned.1.call-done = bf16[576,128]{1,0:T(8,128)(2,1)} async-done(((bf16[4608,128]{1,0:T(8,128)(2,1)}), bf16[576,128]{1,0:T(8,128)(2,1)}) %reduce-scatter.7.cloned.1.call-update) | async-done | bytes 147472
  224.7 1.1 copy.23
  225.8 0.9 copy.21
  226.7 94.2 %all-gather.6.cloned.1.call-done = bf16[1,2048,4608]{2,1,0:T(8,128)(2,1)} async-done(((bf16[1,128,4608]{2,1,0:T(8,128)(2,1)}), bf16[1,2048,4608]{2,1,0:T(8,128)(2,1)}) %all-gather.6.cloned.1.call-update) | async-done | bytes 18874384 | tf_op jit(solution)/shard_map/all_gather | solution.py:22
  320.9 16.1 %multiply_convert_fusion.1 = bf16[512,2048]{1,0:T(8,128)(2,1)} fusion(bf16[512,4608]{1,0:T(8,128)(2,1)} %param.7, bf16[1,2048,4608]{2,1,0:T(8,128)(2,1)} %all-gather.6.cloned.1.call-done), kind=kOutput, calls=%fused_computation.3 | convolution fusion | flops 9665773568 | bytes 25690112 | tf_op jit(solution)/shard_map/dot_general | solution.py:20
  (1 shorter events, 0.0 us)
Async XLA Ops:
  8.0 2.3 copy-start
  8.0 40.8 %all-gather.4.cloned.1.call-start = ((), (), s32[]{:S(2)}) async-start(), calls=%async_computation.2 | async-start | bytes 1327104 | tf_op jit(solution)/shard_map/all_gather | solution.py:10
  10.3 175.2 %reduce-scatter.5.cloned.1.call-start = ((), (), s32[]{:S(2)}) async-start(), calls=%async_computation.3 | async-start | bytes 20054016 | tf_op jit(solution)/shard_map/reduce_scatter | solution.py:30
  25.5 160.0 %copy-start.1 = (bf16[1,128,4608]{2,1,0:T(8,128)(2,1)S(1)}, bf16[1,128,4608]{2,1,0:T(8,128)(2,1)}, u32[]{:S(2)}) copy-start(bf16[1,128,4608]{2,1,0:T(8,128)(2,1)} %param.8) | copy-start | bytes 3538948
  25.5 199.2 %reduce-scatter.7.cloned.1.call-start = ((), (), s32[]{:S(2)}) async-start(), calls=%async_computation.5 | async-start | bytes 1327104
  189.1 3.0 copy-start.2
  191.5 129.4 %all-gather.6.cloned.1.call-start = ((), (), s32[]{:S(2)}) async-start(), calls=%async_computation.4 | async-start | bytes 20054016 | tf_op jit(solution)/shard_map/all_gather | solution.py:22
Sparse Core Ops, SparseCore 0:
  11.2 37.6 all-gather.3
  191.6 33.0 reduce-scatter.6
Sparse Core Ops, SparseCore 1:
  25.6 159.9 reduce-scatter.4
  194.7 126.1 all-gather.5
where the time goes:
time: 345 us; the launch traced here: 344 us
  waiting for transfers between devices  285 us (83%)
  matrix products  31.2 us (9%)
  between operations  15.5 us (4%)
  local copies, waits for them, and re-layouts  7.03 us (2%)
  other arithmetic  5.8 us (2%)
    reduce_scatter x1, waiting for transfers between devices, per_device(): lax.psum_scatter((product_rows * factor).astype(jnp.bfloat16), 'fsdp', sc...  134 us
    all_gather x1, waiting for transfers between devices, per_device(): lax.all_gather(weights, 'fsdp', axis=0, tiled=True)  94.2 us
    unnamed x5, waiting for transfers between devices  33 us
    all_gather x1, waiting for transfers between devices, advance(): lax.all_gather(new_anchor.astype(jnp.bfloat16), 'rep', axis=1, tiled=True)  23.3 us
    dot_general x1, matrix products, per_device(): lax.dot_general(grad_out, lax.all_gather(weights, 'fsdp', axis=0, tiled=T...  16.1 us
    dot_general x1, matrix products, per_device(): lax.dot_general(attn_out, grad_out, (((0,), (0,)), ((), ())), preferred_e...  15.1 us
  transfers between devices with their start and end apart: 4, of which 4 were waited for; matrix products, arithmetic and copies ran while one was open for 6% of the time, Pallas kernels for 0%

commit v1 on v0

v1 whole, which is shorter than its diff:
```python
import functools

import jax
import jax.numpy as jnp
from jax import lax
from jax.experimental import pallas as pl
from jax.experimental.pallas import tpu as pltpu
from jax.sharding import PartitionSpec as P

MESH = pl.DeviceIdType.MESH
BF = jnp.bfloat16
F32 = jnp.float32

BLK = 128
H = 64
TILE_N = 512
TILE_M = 256
PIECE = 576
WIDE = 640

AGX, AGF, AGZ, RS1, RSD, RS2, RSZ, SIBG, SIBA, IG = 0, 4, 6, 14, 18, 22, 26, 28, 29, 30
RAZ, RAY, RRY, RRZ, N_MSG = 38, 39, 45, 57, 59


def kernel(
    a_hbm, g_hbm, w_hbm, anchor_ref, mom_ref, del_ref,
    ig_hbm, ni_ref, na_ref, nm_ref, og_ref,
    w_all, g_all, a_all, a_t, part, rx1, rxd, rx2, rxz,
    ig_own, ig_tx, st, an_all, ry, tz, rzl, pad,
    send, recv, local,
):
    factor = g_hbm.shape[1] ** (-0.5)
    d = g_hbm.shape[1]
    tok = g_hbm.shape[0]
    rep = lax.axis_index("rep")
    fs = lax.axis_index("fsdp")
    x, zh, c = fs // 4, (fs // 2) % 2, fs % 2
    zl, y = rep // 4, rep % 4

    def at_x(k):
        return (x + k) % 4

    def fs_of(xx, zz, cc):
        return xx * 4 + zz * 2 + cc

    sib = (rep, fs_of(x, zh, 1 - c))
    zpeer = (rep, fs_of(x, 1 - zh, c))
    xpeer = {k: (rep, fs_of(at_x(k), zh, c)) for k in (1, 3)}
    ypeer = {k: (zl * 4 + (y + k) % 4, fs) for k in (1, 2, 3)}
    lpeer = ((1 - zl) * 4 + y, fs)

    def blk(k, zi):
        return at_x(k) * 2 + (zh if zi else 1 - zh)

    def msg(i, src, dst, dev):
        return pltpu.make_async_remote_copy(
            src_ref=src, dst_ref=dst, send_sem=send.at[i], recv_sem=recv.at[i],
            device_id=dev, device_id_type=MESH,
        )

    sent = []

    def go(i, src, dst, dev):
        m = msg(i, src, dst, dev)
        m.start()
        sent.append(m)

    def got(i, ref):
        msg(i, ref, ref, sib).wait_recv()

    def rows(h):
        return pl.ds(h * H, H)

    def strips(n, body):
        def step(i, carry):
            body(pl.multiple_of(i * 16, 16))
            return carry

        lax.fori_loop(0, n // 16, step, 0)

    own = blk(0, 1)

    load_g = pltpu.make_async_copy(g_hbm, g_all.at[pl.ds(0, tok)], local.at[0])
    load_a = pltpu.make_async_copy(a_hbm, a_all.at[pl.ds(0, tok)], local.at[1])
    load_w = pltpu.make_async_copy(w_hbm.at[0], w_all.at[own], local.at[2])

    barrier = pltpu.get_barrier_semaphore()
    peers = [sib, zpeer, xpeer[1], xpeer[3], ypeer[1], ypeer[2], ypeer[3], lpeer]
    for p in peers:
        pl.semaphore_signal(barrier, inc=1, device_id=p, device_id_type=MESH)
    load_g.start()
    load_a.start()
    load_w.start()
    pl.semaphore_wait(barrier, len(peers))

    go(SIBA, a_hbm, a_all.at[pl.ds(tok, tok)], sib)
    go(SIBG, g_hbm, g_all.at[pl.ds(tok, tok)], sib)
    for h in (0, 1):
        for way, k in ((0, 1), (1, 3)):
            hh = h if way == 0 else 1 - h
            go(AGX + way * 2 + hh, w_hbm.at[0, rows(hh)], w_all.at[own, rows(hh)], xpeer[k])
        go(AGZ + h, w_hbm.at[0, rows(h)], w_all.at[own, rows(h)], zpeer)

    pad[...] = jnp.zeros_like(pad)

    def outer(r):
        sl = pl.ds(r, 16)
        nm = 0.9 * mom_ref[sl, :] + del_ref[sl, :]
        na = anchor_ref[sl, :] - 0.7 * (del_ref[sl, :] + 0.9 * nm)
        nm_ref[sl, :] = nm
        na_ref[sl, :] = na
        pad[sl, pl.ds(0, PIECE)] = na
        v = pad[sl, :]
        odd = (y % 2) == 1
        an_all[rep, sl, :] = jnp.where(odd, pltpu.roll(v, WIDE - PIECE, 1), v).astype(BF)

    strips(BLK, outer)
    go(RAZ, an_all.at[rep], an_all.at[rep], lpeer)
    for k in (1, 2, 3):
        go(RAY + k - 1, an_all.at[rep], an_all.at[rep], ypeer[k])

    load_a.wait()
    load_g.wait()
    got(SIBA, a_hbm)
    got(SIBG, g_hbm)

    def products(k):
        for zi in (0, 1):
            col = pl.multiple_of(fs_of(at_x(k), zh if zi else 1 - zh, c) * BLK, BLK)
            a_t[pl.ds(zi * BLK, BLK), :] = a_all[:, pl.ds(col, BLK)].T

        def step(n, carry):
            cols = pl.ds(pl.multiple_of(n * TILE_N, TILE_N), TILE_N)
            r = jnp.dot(a_t[...], g_all[:, cols], preferred_element_type=F32) * factor
            part[k, 0, :, cols] = r[:BLK].astype(BF)
            part[k, 1, :, cols] = r[BLK:].astype(BF)
            return carry

        lax.fori_loop(0, d // TILE_N, step, 0)

    def first(zi):
        for h, k in ((0, 1), (1, 3)):
            go(RS1 + zi * 2 + h, part.at[2, zi, rows(h)], rx1.at[zi, h], xpeer[k])

    def direct(zi):
        for h, k in ((1, 1), (0, 3)):
            go(RSD + zi * 2 + h, part.at[k, zi, rows(h)], rxd.at[zi, h], xpeer[k])

    def second(zi):
        for h, k in ((0, 1), (1, 3)):
            got(RS1 + zi * 2 + h, rx1.at[zi, h])

            def body(r, h=h, k=k):
                sl = pl.ds(h * H + r, 16)
                v = part[k, zi, sl, :].astype(F32) + rx1[zi, h, pl.ds(r, 16), :].astype(F32)
                part[k, zi, sl, :] = v.astype(BF)

            strips(H, body)
            go(RS2 + zi * 2 + h, part.at[k, zi, rows(h)], rx2.at[zi, h], xpeer[k])

    def input_grad(slot, k, zi):
        b = blk(k, zi)

        def tile(r):
            sl = pl.ds(r, TILE_M)
            return (
                lax.dot_general(
                    g_all[sl, :], w_all[b], (((1,), (1,)), ((), ())), preferred_element_type=F32
                )
                * factor
            ).astype(BF)

        def to_sib(i, carry):
            r = pl.multiple_of(i * TILE_M, TILE_M)
            ig_tx[slot, pl.ds(r, TILE_M), :] = tile(tok + r)
            return carry

        def to_own(i, carry):
            r = pl.multiple_of(i * TILE_M, TILE_M)
            ig_own[slot, pl.ds(r, TILE_M), :] = tile(r)
            return carry

        col = pl.multiple_of(fs_of(at_x(k), zh if zi else 1 - zh, c) * BLK, BLK)
        there = ig_hbm.at[:, pl.ds(col, BLK)]
        lax.fori_loop(0, tok // TILE_M, to_sib, 0)
        go(IG + slot, ig_tx.at[slot], there, sib)
        lax.fori_loop(0, tok // TILE_M, to_own, 0)
        cp = pltpu.make_async_copy(ig_own.at[slot], there, local.at[3 + slot])
        cp.start()
        stores.append(cp)

    stores = []

    products(2)
    first(0)
    products(1)
    products(3)
    direct(0)

    for way, k in ((0, 3), (1, 1)):
        for h in (0, 1):
            got(AGX + way * 2 + h, w_all.at[blk(k, 1), rows(h)])
            ref = w_all.at[blk(k, 1), rows(h)]
            go(AGZ + 2 + way * 2 + h, ref, ref, zpeer)

    products(0)
    load_w.wait()
    second(0)
    for way, k in ((0, 3), (1, 1)):
        ref = w_all.at[blk(k, 1), rows(way)]
        go(AGF + way, ref, ref, xpeer[1 if way == 0 else 3])
    first(1)
    direct(1)

    got(RAZ, an_all.at[lpeer[0]])
    for k in (1, 2, 3):
        ref = an_all.at[lpeer[0]]
        go(RAY + 3 + k - 1, ref, ref, ypeer[k])

    input_grad(0, 0, 1)
    input_grad(1, 1, 1)
    input_grad(2, 3, 1)

    for h in (0, 1):
        got(RSD + h, rxd.at[0, h])
        got(RS2 + h, rx2.at[0, h])

        def body(r, h=h):
            sl = pl.ds(h * H + r, 16)
            v = (
                part[0, 0, sl, :].astype(F32)
                + rxd[0, h, pl.ds(r, 16), :].astype(F32)
                + rx2[0, h, pl.ds(r, 16), :].astype(F32)
            )
            part[0, 0, sl, :] = v.astype(BF)

        strips(H, body)
        go(RSZ + h, part.at[0, 0, rows(h)], rxz.at[h], zpeer)

    for h in (0, 1):
        ref = w_all.at[blk(2, 1), rows(h)]
        got(AGF + h, ref)
        go(AGZ + 6 + h, ref, ref, zpeer)

    second(1)
    input_grad(3, 2, 1)
    for h in (0, 1):
        got(AGZ + h, w_all.at[blk(0, 0), rows(h)])
    input_grad(4, 0, 0)
    for slot, (way, k) in ((5, (0, 3)), (6, (1, 1))):
        for h in (0, 1):
            got(AGZ + 2 + way * 2 + h, w_all.at[blk(k, 0), rows(h)])
        input_grad(slot, k, 0)

    def piece(zz, yy):
        return pl.multiple_of(zz * 2304 + (yy // 2) * 1152 + (yy % 2) * 512, 128)

    for h in (0, 1):
        got(RSD + 2 + h, rxd.at[1, h])
        got(RSZ + h, rxz.at[h])
        got(RS2 + 2 + h, rx2.at[1, h])

        def body(r, h=h):
            sl = pl.ds(h * H + r, 16)
            hs = pl.ds(r, 16)
            v = (
                (part[0, 1, sl, :].astype(F32) + rxd[1, h, hs, :].astype(F32))
                + rx2[1, h, hs, :].astype(F32)
            ) + rxz[h, hs, :].astype(F32)
            st[sl, :] = (w_all[own, sl, :].astype(F32) - v).astype(BF)

        strips(H, body)
        for k in (1, 2, 3):
            for zz in (0, 1):
                col = piece(zz, (y + k) % 4)
                go(
                    RRY + h * 6 + (k - 1) * 2 + zz,
                    st.at[rows(h), pl.ds(col, WIDE)], ry.at[k - 1, zz, rows(h)], ypeer[k],
                )

    for h in (0, 1):
        got(AGZ + 6 + h, w_all.at[blk(2, 0), rows(h)])
    input_grad(7, 2, 0)

    for k in (1, 2, 3):
        got(RAY + k - 1, an_all.at[rep])
        got(RAY + 3 + k - 1, an_all.at[rep])
    lane = lax.broadcasted_iota(jnp.int32, (16, 128), 1)

    def merge(r):
        sl = pl.ds(r, 16)
        for q in range(4):
            def put(lo, width, v):
                cols = pl.ds(q * 1152 + lo, width)
                ni_ref[0, sl, cols] = (0.5 * v + 0.5 * st[sl, cols].astype(F32)).astype(BF)

            even = an_all[2 * q, sl, :].astype(F32)
            odd = an_all[2 * q + 1, sl, :].astype(F32)
            put(0, 512, even[:, :512])
            put(512, 128, jnp.where(lane < 64, even[:, 512:], odd[:, :128]))
            put(640, 512, odd[:, 128:])

    strips(BLK, merge)

    for h in (0, 1):
        for k in (1, 2, 3):
            for zz in (0, 1):
                got(RRY + h * 6 + (k - 1) * 2 + zz, ry.at[k - 1, zz, rows(h)])

        def total(zz, sl):
            v = st[sl, pl.ds(piece(zz, y), WIDE)].astype(F32)
            for k in range(3):
                v = v + ry[k, zz, sl, :].astype(F32)
            return v

        def give(r, h=h):
            sl = pl.ds(h * H + r, 16)
            tz[sl, :] = total(1 - zl, sl).astype(BF)

        strips(H, give)
        go(RRZ + h, tz.at[rows(h)], rzl.at[rows(h)], lpeer)
    for h in (0, 1):
        got(RRZ + h, rzl.at[rows(h)])

        def finish(r, h=h):
            sl = pl.ds(h * H + r, 16)
            v = total(zl, sl) + rzl[sl, :].astype(F32)
            v = jnp.where((y % 2) == 1, pltpu.roll(v, PIECE, 1), v)
            og_ref[sl, :] = anchor_ref[sl, :] - v[:, :PIECE] * 0.125

        strips(H, finish)

    for slot in range(8):
        got(IG + slot, ig_own.at[slot])
    for cp in stores:
        cp.wait()
    for m in sent:
        m.wait_send()


def per_device(attn_out, grad_out, inner_w, anchor, momentum, delayed):
    tok, d = grad_out.shape
    hd = attn_out.shape[1]
    hbm = pl.BlockSpec(memory_space=pl.ANY)
    vm = pl.BlockSpec(memory_space=pltpu.VMEM)
    shape = jax.ShapeDtypeStruct
    return pl.pallas_call(
        kernel,
        out_shape=(
            shape((tok, hd), BF),
            shape(inner_w.shape, BF),
            shape(anchor.shape, F32),
            shape(anchor.shape, F32),
            shape(anchor.shape, F32),
        ),
        in_specs=[hbm, hbm, hbm, vm, vm, vm],
        out_specs=(hbm, vm, vm, vm, vm),
        scratch_shapes=[
            pltpu.VMEM((8, BLK, d), BF),
            pltpu.VMEM((2 * tok, d), BF),
            pltpu.VMEM((2 * tok, hd), BF),
            pltpu.VMEM((2 * BLK, 2 * tok), BF),
            pltpu.VMEM((4, 2, BLK, d), BF),
            pltpu.VMEM((2, 2, H, d), BF),
            pltpu.VMEM((2, 2, H, d), BF),
            pltpu.VMEM((2, 2, H, d), BF),
            pltpu.VMEM((2, H, d), BF),
            pltpu.VMEM((8, tok, BLK), BF),
            pltpu.VMEM((8, tok, BLK), BF),
            pltpu.VMEM((BLK, d), BF),
            pltpu.VMEM((8, BLK, WIDE), BF),
            pltpu.VMEM((3, 2, BLK, WIDE), BF),
            pltpu.VMEM((BLK, WIDE), BF),
            pltpu.VMEM((BLK, WIDE), BF),
            pltpu.VMEM((BLK, WIDE), F32),
            pltpu.SemaphoreType.DMA((N_MSG,)),
            pltpu.SemaphoreType.DMA((N_MSG,)),
            pltpu.SemaphoreType.DMA((11,)),
        ],
        compiler_params=pltpu.CompilerParams(
            collective_id=0, has_side_effects=True, vmem_limit_bytes=60 * 2**20
        ),
    )(attn_out, grad_out, inner_w, anchor, momentum, delayed)


def solution(mesh):
    return jax.shard_map(
        per_device,
        mesh=mesh,
        in_specs=(
            P(("rep", "fsdp"), None),
            P(("rep", "fsdp"), None),
            P("rep", "fsdp", None),
            P("fsdp", "rep"),
            P("fsdp", "rep"),
            P("fsdp", "rep"),
        ),
        out_specs=(
            P(("rep", "fsdp"), None),
            P("rep", "fsdp", None),
            P("fsdp", "rep"),
            P("fsdp", "rep"),
            P("fsdp", "rep"),
        ),
        check_vma=False,
    )
```

time: 345 us -> 166 us (0.48)
  waiting for transfers between devices: 285 us -> 0 us
  Pallas kernels: 0 us -> 149 us
  matrix products: 31.2 us -> 0 us
  between operations: 15.5 us -> 0.64 us
  local copies, waits for them, and re-layouts: 7.03 us -> 15.3 us
  other arithmetic: 5.8 us -> 0 us
    pallas_call x0 -> x1, Pallas kernels: none -> 149 us  [per_device(): pl.pallas_call(kernel, out_shape=(shape((tok, hd), BF), shape(inner_w.sha...]
    reduce_scatter x1 -> x0, waiting for transfers between devices: 134 us -> none  [per_device(): lax.psum_scatter((product_rows * factor).astype(jnp.bfloat16), 'fsdp', sc...]
    all_gather x2 -> x0, waiting for transfers between devices: 117 us -> none  [the longest x1 94.2 us: per_device(): lax.all_gather(weights, 'fsdp', axis=0, tiled=True)]
    unnamed x5 -> x0, waiting for transfers between devices: 33 us -> none
    dot_general x2 -> x0, matrix products: 31.2 us -> none  [the longest x1 16.1 us: per_device(): lax.dot_general(grad_out, lax.all_gather(weights, 'fsdp', axis=0, tiled=T...]
    pallas_call x0 -> x3, local copies, waits for them, and re-layouts: none -> 5.51 us  [per_device(): pl.pallas_call(kernel, out_shape=(shape((tok, hd), BF), shape(inner_w.sha...]
    unnamed x10 -> x7, local copies, waits for them, and re-layouts: 4.52 us -> 9.83 us
    broadcast_in_dim x1 -> x0, other arithmetic: 3.56 us -> none  [per_device(): return (input_grad, merged[None], new_anchor, new_momentum, outer_grad)]
  transfers between devices with their start and end apart: 4 -> 0, of which waited for: 4 -> 0; matrix products, arithmetic and copies ran while one was open for 6% -> 0% of each run, Pallas kernels for 0% -> 0%
where the time goes in v1:
time: 166 us; the launch traced here: 165 us
  Pallas kernels  149 us (90%)
  local copies, waits for them, and re-layouts  15.3 us (9%)
    pallas_call x1, Pallas kernels, per_device(): pl.pallas_call(kernel, out_shape=(shape((tok, hd), BF), shape(inner_w.sha...  149 us
    unnamed x7, local copies, waits for them, and re-layouts  9.83 us
    pallas_call x3, local copies, waits for them, and re-layouts, per_device(): pl.pallas_call(kernel, out_shape=(shape((tok, hd), BF), shape(inner_w.sha...  5.51 us

profile of v1, /device:TPU:1, one launch (start us, length us, event | category | flops | bytes accessed | tf_op | source)
XLA Modules:
  0.0 164.8 jit_solution(9077954877455988337)
XLA Ops:
  0.6 1.9 %copy.11.anchor_ref = f32[128,576]{1,0:T(8,128)} copy(f32[128,576]{0,1:T(8,128)} %param.9) | data formatting | bytes 589824 | tf_op args[3]
  2.5 1.9 %copy.12.mom_ref = f32[128,576]{1,0:T(8,128)} copy(f32[128,576]{0,1:T(8,128)} %param.10) | data formatting | bytes 589824 | tf_op args[4]
  4.3 1.8 %copy.13.del_ref = f32[128,576]{1,0:T(8,128)} copy(f32[128,576]{0,1:T(8,128)} %param.11) | data formatting | bytes 589824 | tf_op args[5]
  6.2 148.8 %shard_map.101 = (bf16[512,2048]{1,0:T(8,128)(2,1)}, bf16[1,128,4608]{2,1,0:T(8,128)(2,1)}, f32[128,576]{1,0:T(8,128)}, f32[128,576]{1,0:T(8,128)}, f32[128,576]{1,0:T(8,128)}) custom-call(bf16[512,2048]{1,0:T(8,128)(2,1)} %a_hbm.1, bf16[512,4608]{1,0:T(8,128)(2,1)} %g_hbm.1, bf16[1,128,4608]{2,1,0:T(8,128)(2,1)} %w_hbm.1, f32[128,576]{1,0:T(8,128)} %copy.11.anchor_ref, ...), custom_call_target="tpu_custom_call" | custom-call | tf_op jit(solution)/shard_map/pallas_call | solution.py:347
  155.0 1.8 %copy.14 = f32[128,576]{0,1:T(8,128)} copy(f32[128,576]{1,0:T(8,128)} %get-tuple-element.7) | data formatting | bytes 589824 | tf_op jit(solution)/shard_map/pallas_call | solution.py:347
  156.8 1.8 %copy.15 = f32[128,576]{0,1:T(8,128)} copy(f32[128,576]{1,0:T(8,128)} %get-tuple-element.8) | data formatting | bytes 589824 | tf_op jit(solution)/shard_map/pallas_call | solution.py:347
  158.7 1.8 %copy.16 = f32[128,576]{0,1:T(8,128)} copy(f32[128,576]{1,0:T(8,128)} %get-tuple-element.9) | data formatting | bytes 589824 | tf_op jit(solution)/shard_map/pallas_call | solution.py:347
  160.5 0.0 copy-start
  160.5 3.3 %copy.19 = bf16[512,2048]{1,0:T(8,128)(2,1)} copy(bf16[512,2048]{1,0:T(8,128)(2,1)} %get-tuple-element.15) | data formatting | bytes 4194304
  163.8 0.0 copy-done
  163.8 1.0 copy.20
Async XLA Ops:
  160.5 3.3 %copy-start = (bf16[1,128,4608]{2,1,0:T(8,128)(2,1)S(1)}, bf16[1,128,4608]{2,1,0:T(8,128)(2,1)}, u32[]{:S(2)}) copy-start(bf16[1,128,4608]{2,1,0:T(8,128)(2,1)} %get-tuple-element.16) | copy-start | bytes 3538948

commit v2 on v1

v2 whole, which is shorter than its diff:
```python
import functools

import jax
import jax.numpy as jnp
from jax import lax
from jax.experimental import pallas as pl
from jax.experimental.pallas import tpu as pltpu
from jax.sharding import PartitionSpec as P

MESH = pl.DeviceIdType.MESH
BF = jnp.bfloat16
F32 = jnp.float32

BLK = 128
H = 64
NJ = 4
CR = BLK // NJ
HR = CR // 2
TILE_N = 1536
TILE_M = 512
PIECE = 576
WIDE = 640


def numbers(**counts):
    first, at = {}, 0
    for name, count in counts.items():
        first[name] = at
        at += count
    return first, at


FIRST, N_MSG = numbers(
    AGX=4, AGF=4, AGZ=8, AGY=2, RS1=4 * NJ, RSD=4 * NJ, RS2=4 * NJ, RSZ=NJ, SIBG=1, SIBA=1, IG=8,
    RAZ=1, RAY=6, RRY=6 * NJ, RRZ=NJ,
)


def kernel(
    a_hbm, g_hbm, w_hbm, anchor_ref, mom_ref, del_ref,
    ig_hbm, ni_ref, sum_ref,
    w_all, g_all, a_all, a_t, part, rx1, rxd, rx2, rxz,
    ig_own, ig_tx, st, an_all, ry, tz, rzl, total_ref, pad,
    send, recv, local,
):
    d = g_hbm.shape[1]
    tok = g_hbm.shape[0]
    factor = d ** (-0.5)
    rep = lax.axis_index("rep")
    fs = lax.axis_index("fsdp")
    x, zh, c = fs // 4, (fs // 2) % 2, fs % 2
    zl, y = rep // 4, rep % 4

    def at_x(k):
        return (x + k) % 4

    def fs_of(xx, zz, cc):
        return xx * 4 + zz * 2 + cc

    sib = (rep, fs_of(x, zh, 1 - c))
    zpeer = (rep, fs_of(x, 1 - zh, c))
    xpeer = {k: (rep, fs_of(at_x(k), zh, c)) for k in (1, 3)}
    ypeer = {k: (zl * 4 + (y + k) % 4, fs) for k in (1, 2, 3)}
    lpeer = ((1 - zl) * 4 + y, fs)

    def blk(k, zi):
        return at_x(k) * 2 + (zh if zi else 1 - zh)

    def msg(name, i, src, dst, dev):
        n = FIRST[name] + i
        return pltpu.make_async_remote_copy(
            src_ref=src, dst_ref=dst, send_sem=send.at[n], recv_sem=recv.at[n],
            device_id=dev, device_id_type=MESH,
        )

    sent = []

    def go(name, i, src, dst, dev):
        m = msg(name, i, src, dst, dev)
        m.start()
        sent.append(m)

    def got(name, i, ref):
        msg(name, i, ref, ref, sib).wait_recv()

    def half(h):
        return pl.ds(h * H, H)

    def quarter(h, part_of):
        return pl.ds(h * H + part_of * (H // 2), H // 2)

    def chunk(j):
        return pl.ds(j * CR, CR)

    def piece_rows(j, h):
        return pl.ds(j * CR + h * HR, HR)

    own = blk(0, 1)
    shift = pl.multiple_of((y % 2) * (WIDE - PIECE), WIDE - PIECE)

    load_g = pltpu.make_async_copy(g_hbm, g_all.at[pl.ds(0, tok)], local.at[0])
    load_a = pltpu.make_async_copy(a_hbm, a_all.at[pl.ds(0, tok)], local.at[1])
    load_w = pltpu.make_async_copy(w_hbm.at[0], w_all.at[own], local.at[2])

    barrier = pltpu.get_barrier_semaphore()
    peers = [sib, zpeer, xpeer[1], xpeer[3], ypeer[1], ypeer[2], ypeer[3], lpeer]
    for p in peers:
        pl.semaphore_signal(barrier, inc=1, device_id=p, device_id_type=MESH)
    load_g.start()
    load_a.start()
    load_w.start()
    pl.semaphore_wait(barrier, len(peers))

    go("SIBA", 0, a_hbm, a_all.at[pl.ds(tok, tok)], sib)
    go("SIBG", 0, g_hbm, g_all.at[pl.ds(tok, tok)], sib)
    for h in (0, 1):
        for way, k in ((0, 1), (1, 3)):
            hh = h if way == 0 else 1 - h
            go("AGX", way * 2 + hh, w_hbm.at[0, half(hh)], w_all.at[own, half(hh)], xpeer[k])
        go("AGZ", h, w_hbm.at[0, half(h)], w_all.at[own, half(h)], zpeer)

    pad[...] = jnp.zeros_like(pad)
    momentum = 0.9 * mom_ref[...] + del_ref[...]
    pad[pl.ds(shift, PIECE), :] = anchor_ref[...] - 0.7 * (del_ref[...] + 0.9 * momentum)
    an_all[rep] = pad[...].T.astype(BF)
    go("RAZ", 0, an_all.at[rep], an_all.at[rep], lpeer)
    for k in (1, 2, 3):
        go("RAY", k - 1, an_all.at[rep], an_all.at[rep], ypeer[k])

    load_a.wait()
    load_g.wait()
    got("SIBA", 0, a_hbm)
    got("SIBG", 0, g_hbm)

    def products(k):
        for zi in (0, 1):
            col = pl.multiple_of(fs_of(at_x(k), zh if zi else 1 - zh, c) * BLK, BLK)
            a_t[pl.ds(zi * BLK, BLK), :] = a_all[:, pl.ds(col, BLK)].T

        def step(n, carry):
            cols = pl.ds(pl.multiple_of(n * TILE_N, TILE_N), TILE_N)
            r = jnp.dot(a_t[...], g_all[:, cols], preferred_element_type=F32) * factor
            part[k, 0, :, cols] = r[:BLK].astype(BF)
            part[k, 1, :, cols] = r[BLK:].astype(BF)
            return carry

        lax.fori_loop(0, d // TILE_N, step, 0)

    def rs_id(zi, j, h):
        return (zi * NJ + j) * 2 + h

    def first(zi):
        for j in range(NJ):
            for h, k in ((0, 1), (1, 3)):
                go("RS1", rs_id(zi, j, h), part.at[2, zi, piece_rows(j, h)], rx1.at[zi, j, h], xpeer[k])

    def direct(zi, j):
        for h, k in ((1, 1), (0, 3)):
            go("RSD", rs_id(zi, j, h), part.at[k, zi, piece_rows(j, h)], rxd.at[zi, j, h], xpeer[k])

    def second(zi, j):
        for h, k in ((0, 1), (1, 3)):
            got("RS1", rs_id(zi, j, h), rx1.at[zi, j, h])
            sl = piece_rows(j, h)
            v = part[k, zi, sl, :].astype(F32) + rx1[zi, j, h].astype(F32)
            part[k, zi, sl, :] = v.astype(BF)
            go("RS2", rs_id(zi, j, h), part.at[k, zi, sl], rx2.at[zi, j, h], xpeer[k])

    stores = []

    def input_grad(slot, k, zi):
        b = blk(k, zi)

        def tile(r):
            return (
                lax.dot_general(
                    g_all[pl.ds(r, TILE_M), :], w_all[b], (((1,), (1,)), ((), ())),
                    preferred_element_type=F32,
                )
                * factor
            ).astype(BF)

        col = pl.multiple_of(fs_of(at_x(k), zh if zi else 1 - zh, c) * BLK, BLK)
        there = ig_hbm.at[:, pl.ds(col, BLK)]
        for r in range(0, tok, TILE_M):
            ig_tx[slot, pl.ds(r, TILE_M), :] = tile(tok + r)
        go("IG", slot, ig_tx.at[slot], there, sib)
        for r in range(0, tok, TILE_M):
            ig_own[slot, pl.ds(r, TILE_M), :] = tile(r)
        cp = pltpu.make_async_copy(ig_own.at[slot], there, local.at[3 + slot])
        cp.start()
        stores.append(cp)

    products(2)
    first(0)
    products(1)
    products(3)
    for j in range(NJ):
        direct(0, j)
    products(0)
    load_w.wait()

    for way, k in ((0, 3), (1, 1)):
        for h in (0, 1):
            ref = w_all.at[blk(k, 1), half(h)]
            got("AGX", way * 2 + h, ref)
            go("AGZ", 2 + way * 2 + h, ref, ref, zpeer)

    for j in range(NJ):
        second(0, j)
    first(1)

    def onward(part_of):
        for way, k in ((0, 3), (1, 1)):
            ref = w_all.at[blk(k, 1), quarter(way, part_of)]
            go("AGF", way * 2 + part_of, ref, ref, xpeer[1 if way == 0 else 3])

    onward(0)

    got("RAZ", 0, an_all.at[lpeer[0]])
    for k in (1, 2, 3):
        ref = an_all.at[lpeer[0]]
        go("RAY", 3 + k - 1, ref, ref, ypeer[k])

    input_grad(0, 0, 1)
    input_grad(1, 1, 1)
    input_grad(2, 3, 1)

    for j in range(NJ):
        for h in (0, 1):
            got("RSD", rs_id(0, j, h), rxd.at[0, j, h])
            got("RS2", rs_id(0, j, h), rx2.at[0, j, h])
            sl = piece_rows(j, h)
            v = part[0, 0, sl, :].astype(F32) + rxd[0, j, h].astype(F32) + rx2[0, j, h].astype(F32)
            part[0, 0, sl, :] = v.astype(BF)
        go("RSZ", j, part.at[0, 0, chunk(j)], rxz.at[j], zpeer)

    for j in range(NJ):
        direct(1, j)
        second(1, j)
    onward(1)

    for h in (0, 1):
        got("AGZ", h, w_all.at[blk(0, 0), half(h)])
    for way, k in ((0, 3), (1, 1)):
        for h in (0, 1):
            got("AGZ", 2 + way * 2 + h, w_all.at[blk(k, 0), half(h)])
        ref = w_all.at[blk(k, 0), quarter(way, 1)]
        go("AGY", way, ref, ref, xpeer[1 if way == 0 else 3])
    for h in (0, 1):
        ref = w_all.at[blk(2, 1), quarter(h, 0)]
        got("AGF", h * 2, ref)
        go("AGZ", 6 + h, ref, ref, zpeer)
    input_grad(3, 0, 0)
    input_grad(4, 1, 0)

    def piece(zz, yy):
        return pl.multiple_of(zz * 2304 + (yy // 2) * 1152 + (yy % 2) * 512, 128)

    def stepped(j):
        got("RSZ", j, rxz.at[j])
        for h in (0, 1):
            got("RSD", rs_id(1, j, h), rxd.at[1, j, h])
            got("RS2", rs_id(1, j, h), rx2.at[1, j, h])
            sl = piece_rows(j, h)
            v = (part[0, 1, sl, :].astype(F32) + rxd[1, j, h].astype(F32)) + (
                rx2[1, j, h].astype(F32) + rxz[j, pl.ds(h * HR, HR), :].astype(F32)
            )
            st[sl, :] = (w_all[own, sl, :].astype(F32) - v).astype(BF)
        for k in (1, 2, 3):
            for zz in (0, 1):
                col = piece(zz, (y + k) % 4)
                go(
                    "RRY", j * 6 + (k - 1) * 2 + zz,
                    st.at[chunk(j), pl.ds(col, WIDE)], ry.at[k - 1, zz, chunk(j)], ypeer[k],
                )

    def over_y(j):
        for k in (1, 2, 3):
            for zz in (0, 1):
                got("RRY", j * 6 + (k - 1) * 2 + zz, ry.at[k - 1, zz, chunk(j)])

        def total(zz):
            v = st[chunk(j), pl.ds(piece(zz, y), WIDE)].astype(F32)
            for k in range(3):
                v = v + ry[k, zz, chunk(j), :].astype(F32)
            return v

        tz[chunk(j), :] = total(1 - zl).astype(BF)
        go("RRZ", j, tz.at[chunk(j)], rzl.at[chunk(j)], lpeer)
        total_ref[chunk(j), :] = total(zl)

    for j in range(NJ):
        stepped(j)
        if j == 0:
            input_grad(5, 3, 0)
        else:
            over_y(j - 1)

    for k in (1, 2, 3):
        got("RAY", k - 1, an_all.at[rep])
        got("RAY", 3 + k - 1, an_all.at[rep])
    lane = lax.broadcasted_iota(jnp.int32, (16, 128), 1)

    def merge(i, carry):
        sl = pl.ds(pl.multiple_of(i * 16, 16), 16)
        for q in range(4):
            def put(lo, width, v):
                cols = pl.ds(q * 1152 + lo, width)
                ni_ref[0, sl, cols] = (0.5 * v + 0.5 * st[sl, cols].astype(F32)).astype(BF)

            even = an_all[2 * q, sl, :].astype(F32)
            odd = an_all[2 * q + 1, sl, :].astype(F32)
            put(0, 512, even[:, :512])
            put(512, 128, jnp.where(lane < 64, even[:, 512:], odd[:, :128]))
            put(640, 512, odd[:, 128:])
        return carry

    lax.fori_loop(0, BLK // 16, merge, 0)
    over_y(NJ - 1)

    for h in (0, 1):
        got("AGF", h * 2 + 1, w_all.at[blk(2, 1), quarter(h, 1)])
    input_grad(6, 2, 1)

    for j in range(NJ):
        got("RRZ", j, rzl.at[chunk(j)])
    pad[...] = (total_ref[...] + rzl[...].astype(F32)).T
    sum_ref[...] = pad[pl.ds(shift, PIECE), :]

    for h in (0, 1):
        got("AGZ", 6 + h, w_all.at[blk(2, 0), quarter(h, 0)])
        got("AGY", h, w_all.at[blk(2, 0), quarter(h, 1)])
    input_grad(7, 2, 0)

    for slot in range(8):
        got("IG", slot, ig_own.at[slot])
    for cp in stores:
        cp.wait()
    for m in sent:
        m.wait_send()


def per_device(attn_out, grad_out, inner_w, anchor, momentum, delayed):
    tok, d = grad_out.shape
    hd = attn_out.shape[1]
    hbm = pl.BlockSpec(memory_space=pl.ANY)
    vm = pl.BlockSpec(memory_space=pltpu.VMEM)
    shape = jax.ShapeDtypeStruct
    input_grad, new_inner, summed = pl.pallas_call(
        kernel,
        out_shape=(shape((tok, hd), BF), shape(inner_w.shape, BF), shape((PIECE, BLK), F32)),
        in_specs=[hbm, hbm, hbm, vm, vm, vm],
        out_specs=(hbm, vm, vm),
        scratch_shapes=[
            pltpu.VMEM((8, BLK, d), BF),
            pltpu.VMEM((2 * tok, d), BF),
            pltpu.VMEM((2 * tok, hd), BF),
            pltpu.VMEM((2 * BLK, 2 * tok), BF),
            pltpu.VMEM((4, 2, BLK, d), BF),
            pltpu.VMEM((2, NJ, 2, HR, d), BF),
            pltpu.VMEM((2, NJ, 2, HR, d), BF),
            pltpu.VMEM((2, NJ, 2, HR, d), BF),
            pltpu.VMEM((NJ, CR, d), BF),
            pltpu.VMEM((8, tok, BLK), BF),
            pltpu.VMEM((8, tok, BLK), BF),
            pltpu.VMEM((BLK, d), BF),
            pltpu.VMEM((8, BLK, WIDE), BF),
            pltpu.VMEM((3, 2, BLK, WIDE), BF),
            pltpu.VMEM((BLK, WIDE), BF),
            pltpu.VMEM((BLK, WIDE), BF),
            pltpu.VMEM((BLK, WIDE), F32),
            pltpu.VMEM((WIDE, BLK), F32),
            pltpu.SemaphoreType.DMA((N_MSG,)),
            pltpu.SemaphoreType.DMA((N_MSG,)),
            pltpu.SemaphoreType.DMA((11,)),
        ],
        compiler_params=pltpu.CompilerParams(
            collective_id=0, has_side_effects=True, vmem_limit_bytes=60 * 2**20
        ),
    )(attn_out, grad_out, inner_w, anchor.T, momentum.T, delayed.T)
    new_momentum = 0.9 * momentum + delayed
    new_anchor = anchor - 0.7 * (delayed + 0.9 * new_momentum)
    outer_grad = anchor - summed.T / lax.axis_size("rep")
    return (input_grad, new_inner, new_anchor, new_momentum, outer_grad)


def solution(mesh):
    return jax.shard_map(
        per_device,
        mesh=mesh,
        in_specs=(
            P(("rep", "fsdp"), None),
            P(("rep", "fsdp"), None),
            P("rep", "fsdp", None),
            P("fsdp", "rep"),
            P("fsdp", "rep"),
            P("fsdp", "rep"),
        ),
        out_specs=(
            P(("rep", "fsdp"), None),
            P("rep", "fsdp", None),
            P("fsdp", "rep"),
            P("fsdp", "rep"),
            P("fsdp", "rep"),
        ),
        check_vma=False,
    )
```

time: 166 us -> 146 us (0.88)
  local copies, waits for them, and re-layouts: 15.3 us -> 4.28 us
  Pallas kernels: 149 us -> 138 us
  other arithmetic: 0 us -> 1.95 us
    pallas_call x1, Pallas kernels: 149 us -> 138 us  [per_device(): pl.pallas_call(kernel, out_shape=(shape((tok, hd), BF), shape(inner_w.sha...]
    unnamed x7 -> x10, local copies, waits for them, and re-layouts: 9.83 us -> 4.28 us
    pallas_call x3 -> x0, local copies, waits for them, and re-layouts: 5.51 us -> none  [per_device(): pl.pallas_call(kernel, out_shape=(shape((tok, hd), BF), shape(inner_w.sha...]
    sub x0 -> x1, other arithmetic: none -> 1.95 us  [per_device(): new_anchor = anchor - 0.7 * (delayed + 0.9 * new_momentum)]
where the time goes in v2:
time: 146 us; the launch traced here: 145 us
  Pallas kernels  138 us (95%)
  local copies, waits for them, and re-layouts  4.28 us (3%)
  other arithmetic  1.95 us (1%)
    pallas_call x1, Pallas kernels, per_device(): pl.pallas_call(kernel, out_shape=(shape((tok, hd), BF), shape(inner_w.sha...  138 us
    unnamed x10, local copies, waits for them, and re-layouts  4.28 us

profile of v2, /device:TPU:1, one launch (start us, length us, event | category | flops | bytes accessed | tf_op | source)
XLA Modules:
  0.0 144.8 jit_solution(13185435033653175758)
XLA Ops:
  0.6 0.0 copy-start
  0.6 0.0 copy-start.1
  0.7 0.0 copy-start.2
  0.7 137.8 %shard_map.101 = (bf16[512,2048]{1,0:T(8,128)(2,1)}, bf16[1,128,4608]{2,1,0:T(8,128)(2,1)}, f32[576,128]{1,0:T(8,128)}) custom-call(bf16[512,2048]{1,0:T(8,128)(2,1)} %a_hbm.1, bf16[512,4608]{1,0:T(8,128)(2,1)} %g_hbm.1, bf16[1,128,4608]{2,1,0:T(8,128)(2,1)} %w_hbm.1, f32[576,128]{1,0:T(8,128)} %bitcast.5, f32[576,128]{1,0:T(8,128)} %bitcast.6, ...), custom_call_target="tpu_custom_call" | custom-call | tf_op jit(solution)/shard_map/pallas_call | solution.py:350
  138.5 0.0 copy-done
  138.5 0.0 copy-done.1
  138.5 0.0 copy-done.2
  138.5 1.9 %multiply_subtract_fusion = (f32[128,576]{0,1:T(8,128)}, f32[128,576]{0,1:T(8,128)}, f32[128,576]{0,1:T(8,128)}) fusion(f32[128,576]{0,1:T(8,128)S(1)} %copy-done, f32[128,576]{0,1:T(8,128)S(1)} %copy-done.2, f32[128,576]{0,1:T(8,128)S(1)} %copy-done.1, f32[576,128]{1,0:T(8,128)} %get-tuple-element.10), kind=kLoop, calls=%fused_computation.1 | loop fusion | flops 589824 | bytes 2064384 | tf_op jit(solution)/shard_map/sub | solution.py:383
  140.5 0.0 copy-start.3
  140.5 3.3 %copy.13 = bf16[512,2048]{1,0:T(8,128)(2,1)} copy(bf16[512,2048]{1,0:T(8,128)(2,1)} %get-tuple-element.19) | data formatting | bytes 4194304
  143.7 0.0 copy-done.3
  143.7 1.0 copy.14
Async XLA Ops:
  0.6 137.9 %copy-start = (f32[128,576]{0,1:T(8,128)S(1)}, f32[128,576]{0,1:T(8,128)}, u32[]{:S(2)}) copy-start(f32[128,576]{0,1:T(8,128)} %param.9) | copy-start | bytes 884740
  0.6 137.9 %copy-start.1 = (f32[128,576]{0,1:T(8,128)S(1)}, f32[128,576]{0,1:T(8,128)}, u32[]{:S(2)}) copy-start(f32[128,576]{0,1:T(8,128)} %param.10) | copy-start | bytes 884740
  0.7 137.9 %copy-start.2 = (f32[128,576]{0,1:T(8,128)S(1)}, f32[128,576]{0,1:T(8,128)}, u32[]{:S(2)}) copy-start(f32[128,576]{0,1:T(8,128)} %param.11) | copy-start | bytes 884740
  140.5 3.3 %copy-start.3 = (bf16[1,128,4608]{2,1,0:T(8,128)(2,1)S(1)}, bf16[1,128,4608]{2,1,0:T(8,128)(2,1)}, u32[]{:S(2)}) copy-start(bf16[1,128,4608]{2,1,0:T(8,128)(2,1)} %get-tuple-element.20) | copy-start | bytes 3538948

commit v3 on v2

--- a/solution.py
+++ b/solution.py
@@ -18,6 +18,7 @@
 HR = CR // 2
 TILE_N = 1536
 TILE_M = 512
+NQ = 4
 PIECE = 576
 WIDE = 640
 
@@ -31,16 +32,17 @@
 
 
 FIRST, N_MSG = numbers(
-    AGX=4, AGF=4, AGZ=8, AGY=2, RS1=4 * NJ, RSD=4 * NJ, RS2=4 * NJ, RSZ=NJ, SIBG=1, SIBA=1, IG=8,
+    AGX=4, AGF=4, AGZ=8, AGY=2 * NQ, RS1=4 * NJ, RSD=4 * NJ, RS2=4 * NJ, RSZ=NJ, SIBG=1, SIBA=1, IG=8,
     RAZ=1, RAY=6, RRY=6 * NJ, RRZ=NJ,
 )
 
 
 def kernel(
-    a_hbm, g_hbm, w_hbm, anchor_ref, mom_ref, del_ref,
-    ig_hbm, ni_ref, sum_ref,
+    a_hbm, g_hbm, w_hbm, anchor_hbm, mom_hbm, del_hbm,
+    ig_hbm, ni_hbm, sum_hbm,
     w_all, g_all, a_all, a_t, part, rx1, rxd, rx2, rxz,
     ig_own, ig_tx, st, an_all, ry, tz, rzl, total_ref, pad,
+    anchor_ref, mom_ref, del_ref, ni_ref, acc,
     send, recv, local,
 ):
     d = g_hbm.shape[1]
@@ -73,12 +75,14 @@
             device_id=dev, device_id_type=MESH,
         )
 
-    sent = []
+    sent, tail, early = [], [], []
 
     def go(name, i, src, dst, dev):
         m = msg(name, i, src, dst, dev)
         m.start()
         sent.append(m)
+        if name == "AGY":
+            tail.append(m)
 
     def got(name, i, ref):
         msg(name, i, ref, ref, sib).wait_recv()
@@ -101,11 +105,20 @@
     load_g = pltpu.make_async_copy(g_hbm, g_all.at[pl.ds(0, tok)], local.at[0])
     load_a = pltpu.make_async_copy(a_hbm, a_all.at[pl.ds(0, tok)], local.at[1])
     load_w = pltpu.make_async_copy(w_hbm.at[0], w_all.at[own], local.at[2])
+
+    small = [
+        pltpu.make_async_copy(src, dst, local.at[11 + i])
+        for i, (src, dst) in enumerate(
+            ((anchor_hbm, anchor_ref), (mom_hbm, mom_ref), (del_hbm, del_ref))
+        )
+    ]
 
     barrier = pltpu.get_barrier_semaphore()
     peers = [sib, zpeer, xpeer[1], xpeer[3], ypeer[1], ypeer[2], ypeer[3], lpeer]
     for p in peers:
         pl.semaphore_signal(barrier, inc=1, device_id=p, device_id_type=MESH)
+    for cp in small:
+        cp.start()
     load_g.start()
     load_a.start()
     load_w.start()
@@ -120,6 +133,8 @@
         go("AGZ", h, w_hbm.at[0, half(h)], w_all.at[own, half(h)], zpeer)
 
     pad[...] = jnp.zeros_like(pad)
+    for cp in small:
+        cp.wait()
     momentum = 0.9 * mom_ref[...] + del_ref[...]
     pad[pl.ds(shift, PIECE), :] = anchor_ref[...] - 0.7 * (del_ref[...] + 0.9 * momentum)
     an_all[rep] = pad[...].T.astype(BF)
@@ -191,20 +206,23 @@
         cp.start()
         stores.append(cp)
 
+    def to_z(way, h):
+        ref = w_all.at[blk(3 if way == 0 else 1, 1), half(h)]
+        got("AGX", way * 2 + h, ref)
+        go("AGZ", 2 + way * 2 + h, ref, ref, zpeer)
+
     products(2)
     first(0)
     products(1)
+    to_z(0, 0)
+    to_z(1, 1)
     products(3)
     for j in range(NJ):
         direct(0, j)
     products(0)
     load_w.wait()
-
-    for way, k in ((0, 3), (1, 1)):
-        for h in (0, 1):
-            ref = w_all.at[blk(k, 1), half(h)]
-            got("AGX", way * 2 + h, ref)
-            go("AGZ", 2 + way * 2 + h, ref, ref, zpeer)
+    to_z(0, 1)
+    to_z(1, 0)
 
     for j in range(NJ):
         second(0, j)
@@ -242,11 +260,15 @@
 
     for h in (0, 1):
         got("AGZ", h, w_all.at[blk(0, 0), half(h)])
+    later = []
     for way, k in ((0, 3), (1, 1)):
         for h in (0, 1):
             got("AGZ", 2 + way * 2 + h, w_all.at[blk(k, 0), half(h)])
-        ref = w_all.at[blk(k, 0), quarter(way, 1)]
-        go("AGY", way, ref, ref, xpeer[1 if way == 0 else 3])
+        later.append((way, blk(k, 0)))
+    for q in range(NQ):
+        for way, b in later:
+            ref = w_all.at[b, quarter(way, 1), pl.ds(q * (d // NQ), d // NQ)]
+            go("AGY", way * NQ + q, ref, ref, xpeer[1 if way == 0 else 3])
     for h in (0, 1):
         ref = w_all.at[blk(2, 1), quarter(h, 0)]
         got("AGF", h * 2, ref)
@@ -317,6 +339,8 @@
         return carry
 
     lax.fori_loop(0, BLK // 16, merge, 0)
+    merged = pltpu.make_async_copy(ni_ref, ni_hbm, local.at[14])
+    merged.start()
     over_y(NJ - 1)
 
     for h in (0, 1):
@@ -326,32 +350,105 @@
     for j in range(NJ):
         got("RRZ", j, rzl.at[chunk(j)])
     pad[...] = (total_ref[...] + rzl[...].astype(F32)).T
-    sum_ref[...] = pad[pl.ds(shift, PIECE), :]
+    summed = pltpu.make_async_copy(pad.at[pl.ds(shift, PIECE)], sum_hbm, local.at[15])
+    summed.start()
 
     for h in (0, 1):
         got("AGZ", 6 + h, w_all.at[blk(2, 0), quarter(h, 0)])
-        got("AGY", h, w_all.at[blk(2, 0), quarter(h, 1)])
-    input_grad(7, 2, 0)
+    last = blk(2, 0)
+    early.extend(m for m in sent if not any(m is t for t in tail))
+    for m in early:
+        m.wait_send()
+    col = pl.multiple_of(fs_of(at_x(2), 1 - zh, c) * BLK, BLK)
+    there = ig_hbm.at[:, pl.ds(col, BLK)]
+    for q in range(NQ):
+        cols = pl.ds(q * (d // NQ), d // NQ)
+        for way in (0, 1):
+            got("AGY", way * NQ + q, w_all.at[last, quarter(way, 1), cols])
+        for r in (1, 0):
+            sl = pl.ds(r * tok, tok)
+            v = lax.dot_general(
+                g_all[sl, cols], w_all[last, :, cols], (((1,), (1,)), ((), ())),
+                preferred_element_type=F32,
+            )
+            if q > 0:
+                v = v + acc[sl, :]
+            if q < NQ - 1:
+                acc[sl, :] = v
+            elif r:
+                ig_tx[7] = (v * factor).astype(BF)
+                go("IG", 7, ig_tx.at[7], there, sib)
+            else:
+                ig_own[7] = (v * factor).astype(BF)
+    cp = pltpu.make_async_copy(ig_own.at[7], there, local.at[10])
+    cp.start()
+    stores.append(cp)
 
     for slot in range(8):
         got("IG", slot, ig_own.at[slot])
-    for cp in stores:
+    for cp in stores + [merged, summed]:
         cp.wait()
-    for m in sent:
+    for m in sent[len(early) + len(tail):] + tail:
         m.wait_send()
+
+
+def finish(
+    ig, ni, total, anchor, mom, delayed, ig_out, ni_out, na_out, nm_out, og_out,
+    ig_v, ni_v, total_v, anchor_v, mom_v, del_v, na_v, nm_v, og_v, sem,
+):
+    copy = pltpu.make_async_copy
+    pieces = [(total, total_v), (anchor, anchor_v), (mom, mom_v), (delayed, del_v)]
+    loads = [copy(a, b, sem.at[i]) for i, (a, b) in enumerate(pieces)]
+    n = len(loads)
+    out = []
+    rows = ig.shape[0] // 4
+    for i in range(4):
+        sl = pl.ds(i * rows, rows)
+        out.append((ig.at[sl], ig_v.at[sl], ig_out.at[sl]))
+    for i in range(2):
+        sl = pl.ds(i * H, H)
+        out.append((ni.at[0, sl], ni_v.at[sl], ni_out.at[0, sl]))
+    through = [
+        (copy(a, b, sem.at[n + i]), copy(b, c, sem.at[n + len(out) + i]))
+        for i, (a, b, c) in enumerate(out)
+    ]
+    for cp in loads:
+        cp.start()
+    for cp, _ in through:
+        cp.start()
+    for cp in loads:
+        cp.wait()
+    momentum = 0.9 * mom_v[...] + del_v[...]
+    nm_v[...] = momentum
+    na_v[...] = anchor_v[...] - 0.7 * (del_v[...] + 0.9 * momentum)
+    og_v[...] = anchor_v[...] - total_v[...] * 0.125
+    n += 2 * len(out)
+    done = [
+        copy(a, b, sem.at[n + i])
+        for i, (a, b) in enumerate(((nm_v, nm_out), (na_v, na_out), (og_v, og_out)))
+    ]
+    for cp in done:
+        cp.start()
+    for first, second in through:
+        first.wait()
+        second.start()
+    for cp in done:
+        cp.wait()
+    for _, second in through:
+        second.wait()
 
 
 def per_device(attn_out, grad_out, inner_w, anchor, momentum, delayed):
     tok, d = grad_out.shape
     hd = attn_out.shape[1]
     hbm = pl.BlockSpec(memory_space=pl.ANY)
-    vm = pl.BlockSpec(memory_space=pltpu.VMEM)
     shape = jax.ShapeDtypeStruct
+    across = (anchor.T, momentum.T, delayed.T)
     input_grad, new_inner, summed = pl.pallas_call(
         kernel,
         out_shape=(shape((tok, hd), BF), shape(inner_w.shape, BF), shape((PIECE, BLK), F32)),
-        in_specs=[hbm, hbm, hbm, vm, vm, vm],
-        out_specs=(hbm, vm, vm),
+        in_specs=[hbm] * 6,
+        out_specs=(hbm,) * 3,
         scratch_shapes=[
             pltpu.VMEM((8, BLK, d), BF),
             pltpu.VMEM((2 * tok, d), BF),
@@ -371,18 +468,31 @@
             pltpu.VMEM((BLK, WIDE), BF),
             pltpu.VMEM((BLK, WIDE), F32),
             pltpu.VMEM((WIDE, BLK), F32),
+            pltpu.VMEM((PIECE, BLK), F32),
+            pltpu.VMEM((PIECE, BLK), F32),
+            pltpu.VMEM((PIECE, BLK), F32),
+            pltpu.VMEM((1, BLK, d), BF),
+            pltpu.VMEM((2 * tok, BLK), F32),
             pltpu.SemaphoreType.DMA((N_MSG,)),
             pltpu.SemaphoreType.DMA((N_MSG,)),
-            pltpu.SemaphoreType.DMA((11,)),
+            pltpu.SemaphoreType.DMA((16,)),
         ],
         compiler_params=pltpu.CompilerParams(
             collective_id=0, has_side_effects=True, vmem_limit_bytes=60 * 2**20
         ),
-    )(attn_out, grad_out, inner_w, anchor.T, momentum.T, delayed.T)
-    new_momentum = 0.9 * momentum + delayed
-    new_anchor = anchor - 0.7 * (delayed + 0.9 * new_momentum)
-    outer_grad = anchor - summed.T / lax.axis_size("rep")
-    return (input_grad, new_inner, new_anchor, new_momentum, outer_grad)
+    )(attn_out, grad_out, inner_w, *across)
+    f32 = shape((PIECE, BLK), F32)
+    input_grad, new_inner, *rest = pl.pallas_call(
+        finish,
+        out_shape=(shape((tok, hd), BF), shape(inner_w.shape, BF), f32, f32, f32),
+        in_specs=[hbm] * 6,
+        out_specs=(hbm,) * 5,
+        scratch_shapes=[pltpu.VMEM((tok, hd), BF), pltpu.VMEM((BLK, d), BF)]
+        + [pltpu.VMEM((PIECE, BLK), F32)] * 7
+        + [pltpu.SemaphoreType.DMA((19,))],
+        compiler_params=pltpu.CompilerParams(vmem_limit_bytes=60 * 2**20),
+    )(input_grad, new_inner, summed, *across)
+    return (input_grad, new_inner, *(v.T for v in rest))
 
 
 def solution(mesh):

time: 146 us -> 140 us (0.959); the launches traced: 145 us -> 140 us
  local copies, waits for them, and re-layouts: 4.28 us -> 0 us
  Pallas kernels: 138 us -> 140 us
  other arithmetic: 1.95 us -> 0 us
    unnamed x10 -> x0, local copies, waits for them, and re-layouts: 4.28 us -> none
    pallas_call x0 -> x1, Pallas kernels: none -> 3.46 us  [per_device(): pl.pallas_call(finish, out_shape=(shape((tok, hd), BF), shape(inner_w.sha...]
    sub x1 -> x0, other arithmetic: 1.95 us -> none  [per_device(): new_anchor = anchor - 0.7 * (delayed + 0.9 * new_momentum)]
    pallas_call x1, Pallas kernels: 138 us -> 136 us  [per_device(): pl.pallas_call(kernel, out_shape=(shape((tok, hd), BF), shape(inner_w.sha...]
where the time goes in v3:
time: 140 us
  Pallas kernels  140 us (100%)
    pallas_call x1, Pallas kernels, per_device(): pl.pallas_call(kernel, out_shape=(shape((tok, hd), BF), shape(inner_w.sha...  136 us
    pallas_call x1, Pallas kernels, per_device(): pl.pallas_call(finish, out_shape=(shape((tok, hd), BF), shape(inner_w.sha...  3.46 us

profile of v3, /device:TPU:1, one launch (start us, length us, event | category | flops | bytes accessed | tf_op | source)
XLA Modules:
  0.0 140.3 jit_solution(2837962844197634641)
XLA Ops:
  0.6 136.1 %shard_map.101 = (bf16[512,2048]{1,0:T(8,128)(2,1)}, bf16[1,128,4608]{2,1,0:T(8,128)(2,1)}, f32[576,128]{1,0:T(8,128)}) custom-call(bf16[512,2048]{1,0:T(8,128)(2,1)} %a_hbm.1, bf16[512,4608]{1,0:T(8,128)(2,1)} %g_hbm.1, bf16[1,128,4608]{2,1,0:T(8,128)(2,1)} %w_hbm.1, f32[576,128]{1,0:T(8,128)} %bitcast.6, f32[576,128]{1,0:T(8,128)} %bitcast.8, ...), custom_call_target="tpu_custom_call" | custom-call | tf_op jit(solution)/shard_map/pallas_call | solution.py:447
  136.7 3.5 %shard_map.102 = (bf16[512,2048]{1,0:T(8,128)(2,1)}, bf16[1,128,4608]{2,1,0:T(8,128)(2,1)}, f32[576,128]{1,0:T(8,128)}, f32[576,128]{1,0:T(8,128)}, f32[576,128]{1,0:T(8,128)}) custom-call(bf16[512,2048]{1,0:T(8,128)(2,1)} %get-tuple-element.13.ig, bf16[1,128,4608]{2,1,0:T(8,128)(2,1)} %get-tuple-element.14.ni, f32[576,128]{1,0:T(8,128)} %get-tuple-element.15.total, ...), custom_call_target="tpu_custom_call" | custom-call | tf_op jit(solution)/shard_map/pallas_call | solution.py:485

commit v4 on v3

--- a/solution.py
+++ b/solution.py
@@ -39,10 +39,10 @@
 
 def kernel(
     a_hbm, g_hbm, w_hbm, anchor_hbm, mom_hbm, del_hbm,
-    ig_hbm, ni_hbm, sum_hbm,
+    ig_ref, ni_ref, sum_ref,
     w_all, g_all, a_all, a_t, part, rx1, rxd, rx2, rxz,
-    ig_own, ig_tx, st, an_all, ry, tz, rzl, total_ref, pad,
-    anchor_ref, mom_ref, del_ref, ni_ref, acc,
+    ig_tx, st, an_all, ry, tz, rzl, total_ref, pad,
+    anchor_ref, mom_ref, del_ref, acc,
     send, recv, local,
 ):
     d = g_hbm.shape[1]
@@ -107,7 +107,7 @@
     load_w = pltpu.make_async_copy(w_hbm.at[0], w_all.at[own], local.at[2])
 
     small = [
-        pltpu.make_async_copy(src, dst, local.at[11 + i])
+        pltpu.make_async_copy(src, dst, local.at[3 + i])
         for i, (src, dst) in enumerate(
             ((anchor_hbm, anchor_ref), (mom_hbm, mom_ref), (del_hbm, del_ref))
         )
@@ -181,8 +181,6 @@
             part[k, zi, sl, :] = v.astype(BF)
             go("RS2", rs_id(zi, j, h), part.at[k, zi, sl], rx2.at[zi, j, h], xpeer[k])
 
-    stores = []
-
     def input_grad(slot, k, zi):
         b = blk(k, zi)
 
@@ -196,15 +194,12 @@
             ).astype(BF)
 
         col = pl.multiple_of(fs_of(at_x(k), zh if zi else 1 - zh, c) * BLK, BLK)
-        there = ig_hbm.at[:, pl.ds(col, BLK)]
+        there = ig_ref.at[:, pl.ds(col, BLK)]
         for r in range(0, tok, TILE_M):
             ig_tx[slot, pl.ds(r, TILE_M), :] = tile(tok + r)
         go("IG", slot, ig_tx.at[slot], there, sib)
         for r in range(0, tok, TILE_M):
-            ig_own[slot, pl.ds(r, TILE_M), :] = tile(r)
-        cp = pltpu.make_async_copy(ig_own.at[slot], there, local.at[3 + slot])
-        cp.start()
-        stores.append(cp)
+            ig_ref[pl.ds(r, TILE_M), pl.ds(col, BLK)] = tile(r)
 
     def to_z(way, h):
         ref = w_all.at[blk(3 if way == 0 else 1, 1), half(h)]
@@ -339,8 +334,6 @@
         return carry
 
     lax.fori_loop(0, BLK // 16, merge, 0)
-    merged = pltpu.make_async_copy(ni_ref, ni_hbm, local.at[14])
-    merged.start()
     over_y(NJ - 1)
 
     for h in (0, 1):
@@ -350,8 +343,7 @@
     for j in range(NJ):
         got("RRZ", j, rzl.at[chunk(j)])
     pad[...] = (total_ref[...] + rzl[...].astype(F32)).T
-    summed = pltpu.make_async_copy(pad.at[pl.ds(shift, PIECE)], sum_hbm, local.at[15])
-    summed.start()
+    sum_ref[...] = pad[pl.ds(shift, PIECE), :]
 
     for h in (0, 1):
         got("AGZ", 6 + h, w_all.at[blk(2, 0), quarter(h, 0)])
@@ -360,7 +352,7 @@
     for m in early:
         m.wait_send()
     col = pl.multiple_of(fs_of(at_x(2), 1 - zh, c) * BLK, BLK)
-    there = ig_hbm.at[:, pl.ds(col, BLK)]
+    there = ig_ref.at[:, pl.ds(col, BLK)]
     for q in range(NQ):
         cols = pl.ds(q * (d // NQ), d // NQ)
         for way in (0, 1):
@@ -379,76 +371,51 @@
                 ig_tx[7] = (v * factor).astype(BF)
                 go("IG", 7, ig_tx.at[7], there, sib)
             else:
-                ig_own[7] = (v * factor).astype(BF)
-    cp = pltpu.make_async_copy(ig_own.at[7], there, local.at[10])
-    cp.start()
-    stores.append(cp)
+                ig_ref[:, pl.ds(col, BLK)] = (v * factor).astype(BF)
 
     for slot in range(8):
-        got("IG", slot, ig_own.at[slot])
-    for cp in stores + [merged, summed]:
-        cp.wait()
+        got("IG", slot, ig_tx.at[slot])
     for m in sent[len(early) + len(tail):] + tail:
         m.wait_send()
 
 
 def finish(
     ig, ni, total, anchor, mom, delayed, ig_out, ni_out, na_out, nm_out, og_out,
-    ig_v, ni_v, total_v, anchor_v, mom_v, del_v, na_v, nm_v, og_v, sem,
+    na_v, nm_v, og_v, sem,
 ):
-    copy = pltpu.make_async_copy
-    pieces = [(total, total_v), (anchor, anchor_v), (mom, mom_v), (delayed, del_v)]
-    loads = [copy(a, b, sem.at[i]) for i, (a, b) in enumerate(pieces)]
-    n = len(loads)
-    out = []
-    rows = ig.shape[0] // 4
-    for i in range(4):
-        sl = pl.ds(i * rows, rows)
-        out.append((ig.at[sl], ig_v.at[sl], ig_out.at[sl]))
-    for i in range(2):
-        sl = pl.ds(i * H, H)
-        out.append((ni.at[0, sl], ni_v.at[sl], ni_out.at[0, sl]))
-    through = [
-        (copy(a, b, sem.at[n + i]), copy(b, c, sem.at[n + len(out) + i]))
-        for i, (a, b, c) in enumerate(out)
+    copies = [
+        pltpu.make_async_copy(a, b, sem.at[i])
+        for i, (a, b) in enumerate(
+            ((ig, ig_out), (ni, ni_out), (nm_v, nm_out), (na_v, na_out), (og_v, og_out))
+        )
     ]
-    for cp in loads:
-        cp.start()
-    for cp, _ in through:
-        cp.start()
-    for cp in loads:
+    copies[0].start()
+    copies[1].start()
+    momentum = 0.9 * mom[...] + delayed[...]
+    nm_v[...] = momentum
+    copies[2].start()
+    na_v[...] = anchor[...] - 0.7 * (delayed[...] + 0.9 * momentum)
+    copies[3].start()
+    og_v[...] = anchor[...] - total[...] * 0.125
+    copies[4].start()
+    for cp in copies:
         cp.wait()
-    momentum = 0.9 * mom_v[...] + del_v[...]
-    nm_v[...] = momentum
-    na_v[...] = anchor_v[...] - 0.7 * (del_v[...] + 0.9 * momentum)
-    og_v[...] = anchor_v[...] - total_v[...] * 0.125
-    n += 2 * len(out)
-    done = [
-        copy(a, b, sem.at[n + i])
-        for i, (a, b) in enumerate(((nm_v, nm_out), (na_v, na_out), (og_v, og_out)))
-    ]
-    for cp in done:
-        cp.start()
-    for first, second in through:
-        first.wait()
-        second.start()
-    for cp in done:
-        cp.wait()
-    for _, second in through:
-        second.wait()
 
 
 def per_device(attn_out, grad_out, inner_w, anchor, momentum, delayed):
     tok, d = grad_out.shape
     hd = attn_out.shape[1]
     hbm = pl.BlockSpec(memory_space=pl.ANY)
+    vm = pl.BlockSpec(memory_space=pltpu.VMEM)
     shape = jax.ShapeDtypeStruct
     across = (anchor.T, momentum.T, delayed.T)
     input_grad, new_inner, summed = pl.pallas_call(
         kernel,
-        out_shape=(shape((tok, hd), BF), shape(inner_w.shape, BF), shape((PIECE, BLK), F32)),
+        out_shape=(
+            pltpu.VMEM((tok, hd), BF), pltpu.VMEM(inner_w.shape, BF), pltpu.VMEM((PIECE, BLK), F32)
+        ),
         in_specs=[hbm] * 6,
-        out_specs=(hbm,) * 3,
+        out_specs=(vm,) * 3,
         scratch_shapes=[
             pltpu.VMEM((8, BLK, d), BF),
             pltpu.VMEM((2 * tok, d), BF),
@@ -460,7 +427,6 @@
             pltpu.VMEM((2, NJ, 2, HR, d), BF),
             pltpu.VMEM((NJ, CR, d), BF),
             pltpu.VMEM((8, tok, BLK), BF),
-            pltpu.VMEM((8, tok, BLK), BF),
             pltpu.VMEM((BLK, d), BF),
             pltpu.VMEM((8, BLK, WIDE), BF),
             pltpu.VMEM((3, 2, BLK, WIDE), BF),
@@ -471,26 +437,23 @@
             pltpu.VMEM((PIECE, BLK), F32),
             pltpu.VMEM((PIECE, BLK), F32),
             pltpu.VMEM((PIECE, BLK), F32),
-            pltpu.VMEM((1, BLK, d), BF),
             pltpu.VMEM((2 * tok, BLK), F32),
             pltpu.SemaphoreType.DMA((N_MSG,)),
             pltpu.SemaphoreType.DMA((N_MSG,)),
-            pltpu.SemaphoreType.DMA((16,)),
+            pltpu.SemaphoreType.DMA((6,)),
         ],
         compiler_params=pltpu.CompilerParams(
-            collective_id=0, has_side_effects=True, vmem_limit_bytes=60 * 2**20
+            collective_id=0, has_side_effects=True, vmem_limit_bytes=57 * 2**20
         ),
     )(attn_out, grad_out, inner_w, *across)
     f32 = shape((PIECE, BLK), F32)
     input_grad, new_inner, *rest = pl.pallas_call(
         finish,
         out_shape=(shape((tok, hd), BF), shape(inner_w.shape, BF), f32, f32, f32),
-        in_specs=[hbm] * 6,
+        in_specs=[vm] * 6,
         out_specs=(hbm,) * 5,
-        scratch_shapes=[pltpu.VMEM((tok, hd), BF), pltpu.VMEM((BLK, d), BF)]
-        + [pltpu.VMEM((PIECE, BLK), F32)] * 7
-        + [pltpu.SemaphoreType.DMA((19,))],
-        compiler_params=pltpu.CompilerParams(vmem_limit_bytes=60 * 2**20),
+        scratch_shapes=[pltpu.VMEM((PIECE, BLK), F32)] * 3 + [pltpu.SemaphoreType.DMA((5,))],
+        compiler_params=pltpu.CompilerParams(vmem_limit_bytes=16 * 2**20),
     )(input_grad, new_inner, summed, *across)
     return (input_grad, new_inner, *(v.T for v in rest))
 

time: 140 us -> 139 us (level)
  Pallas kernels: 140 us -> 138 us
    pallas_call x1, Pallas kernels: 3.46 us -> 2.03 us  [per_device(): pl.pallas_call(finish, out_shape=(shape((tok, hd), BF), shape(inner_w.sha...]
where the time goes in v4:
time: 139 us
  Pallas kernels  138 us (99%)
    pallas_call x1, Pallas kernels, per_device(): pl.pallas_call(kernel, out_shape=(pltpu.VMEM((tok, hd), BF), pltpu.VMEM(i...  136 us

profile of v4, /device:TPU:1, one launch (start us, length us, event | category | flops | bytes accessed | tf_op | source)
XLA Modules:
  0.0 138.8 jit_solution(18109308896067882457)
XLA Ops:
  0.6 0.0 copy-start
  0.6 0.0 copy-start.1
  0.7 0.0 copy-start.2
  0.7 135.8 %shard_map.101 = (bf16[512,2048]{1,0:T(8,128)(2,1)S(1)}, bf16[1,128,4608]{2,1,0:T(8,128)(2,1)S(1)}, f32[576,128]{1,0:T(8,128)S(1)}) custom-call(bf16[512,2048]{1,0:T(8,128)(2,1)} %a_hbm.1, bf16[512,4608]{1,0:T(8,128)(2,1)} %g_hbm.1, bf16[1,128,4608]{2,1,0:T(8,128)(2,1)} %w_hbm.1, f32[576,128]{1,0:T(8,128)} %bitcast.6, f32[576,128]{1,0:T(8,128)} %bitcast.8, ...), custom_call_target="tpu_custom_call" | custom-call | tf_op jit(solution)/shard_map/pallas_call | solution.py:412
  136.5 0.0 copy-done
  136.5 0.0 copy-done.1
  136.5 0.0 copy-done.2
  136.5 2.0 %shard_map.102 = (bf16[512,2048]{1,0:T(8,128)(2,1)}, bf16[1,128,4608]{2,1,0:T(8,128)(2,1)}, f32[576,128]{1,0:T(8,128)}, f32[576,128]{1,0:T(8,128)}, f32[576,128]{1,0:T(8,128)}) custom-call(bf16[512,2048]{1,0:T(8,128)(2,1)S(1)} %get-tuple-element.13.ig, bf16[1,128,4608]{2,1,0:T(8,128)(2,1)S(1)} %get-tuple-element.14.ni, ...), custom_call_target="tpu_custom_call" | custom-call | tf_op jit(solution)/shard_map/pallas_call | solution.py:450
Async XLA Ops:
  0.6 135.9 %copy-start = (f32[128,576]{0,1:T(8,128)S(1)}, f32[128,576]{0,1:T(8,128)}, u32[]{:S(2)}) copy-start(f32[128,576]{0,1:T(8,128)} %param.9) | copy-start | bytes 884740
  0.6 135.9 %copy-start.1 = (f32[128,576]{0,1:T(8,128)S(1)}, f32[128,576]{0,1:T(8,128)}, u32[]{:S(2)}) copy-start(f32[128,576]{0,1:T(8,128)} %param.10) | copy-start | bytes 884740
  0.7 135.9 %copy-start.2 = (f32[128,576]{0,1:T(8,128)S(1)}, f32[128,576]{0,1:T(8,128)}, u32[]{:S(2)}) copy-start(f32[128,576]{0,1:T(8,128)} %param.11) | copy-start | bytes 884740

commit v5 on v4

--- a/solution.py
+++ b/solution.py
@@ -75,14 +75,23 @@
             device_id=dev, device_id_type=MESH,
         )
 
-    sent, tail, early = [], [], []
+    sent, late = [], []
+
+    def rs_id(zi, j, h):
+        return (zi * NJ + j) * 2 + h
 
     def go(name, i, src, dst, dev):
         m = msg(name, i, src, dst, dev)
         m.start()
-        sent.append(m)
-        if name == "AGY":
-            tail.append(m)
+        last = (
+            name in ("AGY", "RRZ")
+            or (name == "AGZ" and i >= 6)
+            or (name == "AGF" and i % 2 == 1)
+            or (name == "RRY" and i >= 6 * (NJ - 1))
+            or (name in ("RSD", "RS2") and i >= rs_id(1, NJ - 1, 0))
+            or (name == "IG" and i >= 5)
+        )
+        (late if last else sent).append(m)
 
     def got(name, i, ref):
         msg(name, i, ref, ref, sib).wait_recv()
@@ -160,9 +169,6 @@
             return carry
 
         lax.fori_loop(0, d // TILE_N, step, 0)
-
-    def rs_id(zi, j, h):
-        return (zi * NJ + j) * 2 + h
 
     def first(zi):
         for j in range(NJ):
@@ -334,23 +340,17 @@
         return carry
 
     lax.fori_loop(0, BLK // 16, merge, 0)
+    for m in sent:
+        m.wait_send()
     over_y(NJ - 1)
 
     for h in (0, 1):
         got("AGF", h * 2 + 1, w_all.at[blk(2, 1), quarter(h, 1)])
     input_grad(6, 2, 1)
 
-    for j in range(NJ):
-        got("RRZ", j, rzl.at[chunk(j)])
-    pad[...] = (total_ref[...] + rzl[...].astype(F32)).T
-    sum_ref[...] = pad[pl.ds(shift, PIECE), :]
-
     for h in (0, 1):
         got("AGZ", 6 + h, w_all.at[blk(2, 0), quarter(h, 0)])
     last = blk(2, 0)
-    early.extend(m for m in sent if not any(m is t for t in tail))
-    for m in early:
-        m.wait_send()
     col = pl.multiple_of(fs_of(at_x(2), 1 - zh, c) * BLK, BLK)
     there = ig_ref.at[:, pl.ds(col, BLK)]
     for q in range(NQ):
@@ -373,9 +373,14 @@
             else:
                 ig_ref[:, pl.ds(col, BLK)] = (v * factor).astype(BF)
 
+    for j in range(NJ):
+        got("RRZ", j, rzl.at[chunk(j)])
+    pad[...] = (total_ref[...] + rzl[...].astype(F32)).T
+    sum_ref[...] = pad[pl.ds(shift, PIECE), :]
+
     for slot in range(8):
         got("IG", slot, ig_tx.at[slot])
-    for m in sent[len(early) + len(tail):] + tail:
+    for m in late:
         m.wait_send()
 
 

time: 139 us -> 139 us (level)
  no operation moved by 1% of the time
where the time goes in v5:
time: 139 us; the launch traced here: 138 us
  Pallas kernels  138 us (99%)
    pallas_call x1, Pallas kernels, per_device(): pl.pallas_call(kernel, out_shape=(pltpu.VMEM((tok, hd), BF), pltpu.VMEM(i...  135 us

profile of v5, /device:TPU:1, one launch (start us, length us, event | category | flops | bytes accessed | tf_op | source)
XLA Modules:
  0.0 138.4 jit_solution(15311289391924843156)
XLA Ops:
  0.6 0.0 copy-start
  0.6 0.0 copy-start.1
  0.7 0.0 copy-start.2
  0.7 135.5 %shard_map.101 = (bf16[512,2048]{1,0:T(8,128)(2,1)S(1)}, bf16[1,128,4608]{2,1,0:T(8,128)(2,1)S(1)}, f32[576,128]{1,0:T(8,128)S(1)}) custom-call(bf16[512,2048]{1,0:T(8,128)(2,1)} %a_hbm.1, bf16[512,4608]{1,0:T(8,128)(2,1)} %g_hbm.1, bf16[1,128,4608]{2,1,0:T(8,128)(2,1)} %w_hbm.1, f32[576,128]{1,0:T(8,128)} %bitcast.6, f32[576,128]{1,0:T(8,128)} %bitcast.8, ...), custom_call_target="tpu_custom_call" | custom-call | tf_op jit(solution)/shard_map/pallas_call | solution.py:417
  136.2 0.0 copy-done
  136.2 0.0 copy-done.1
  136.2 0.0 copy-done.2
  136.2 2.0 %shard_map.102 = (bf16[512,2048]{1,0:T(8,128)(2,1)}, bf16[1,128,4608]{2,1,0:T(8,128)(2,1)}, f32[576,128]{1,0:T(8,128)}, f32[576,128]{1,0:T(8,128)}, f32[576,128]{1,0:T(8,128)}) custom-call(bf16[512,2048]{1,0:T(8,128)(2,1)S(1)} %get-tuple-element.13.ig, bf16[1,128,4608]{2,1,0:T(8,128)(2,1)S(1)} %get-tuple-element.14.ni, ...), custom_call_target="tpu_custom_call" | custom-call | tf_op jit(solution)/shard_map/pallas_call | solution.py:455
Async XLA Ops:
  0.6 135.5 %copy-start = (f32[128,576]{0,1:T(8,128)S(1)}, f32[128,576]{0,1:T(8,128)}, u32[]{:S(2)}) copy-start(f32[128,576]{0,1:T(8,128)} %param.9) | copy-start | bytes 884740
  0.6 135.5 %copy-start.1 = (f32[128,576]{0,1:T(8,128)S(1)}, f32[128,576]{0,1:T(8,128)}, u32[]{:S(2)}) copy-start(f32[128,576]{0,1:T(8,128)} %param.10) | copy-start | bytes 884740
  0.7 135.5 %copy-start.2 = (f32[128,576]{0,1:T(8,128)S(1)}, f32[128,576]{0,1:T(8,128)}, u32[]{:S(2)}) copy-start(f32[128,576]{0,1:T(8,128)} %param.11) | copy-start | bytes 884740

commit v6 on v5

--- a/solution.py
+++ b/solution.py
@@ -346,13 +346,11 @@
 
     for h in (0, 1):
         got("AGF", h * 2 + 1, w_all.at[blk(2, 1), quarter(h, 1)])
-    input_grad(6, 2, 1)
 
     for h in (0, 1):
         got("AGZ", 6 + h, w_all.at[blk(2, 0), quarter(h, 0)])
     last = blk(2, 0)
-    col = pl.multiple_of(fs_of(at_x(2), 1 - zh, c) * BLK, BLK)
-    there = ig_ref.at[:, pl.ds(col, BLK)]
+    pair = pl.ds(at_x(2) * 2, 2)
     for q in range(NQ):
         cols = pl.ds(q * (d // NQ), d // NQ)
         for way in (0, 1):
@@ -360,18 +358,23 @@
         for r in (1, 0):
             sl = pl.ds(r * tok, tok)
             v = lax.dot_general(
-                g_all[sl, cols], w_all[last, :, cols], (((1,), (1,)), ((), ())),
-                preferred_element_type=F32,
+                g_all[sl, cols], w_all[pair, :, cols].reshape(2 * BLK, d // NQ),
+                (((1,), (1,)), ((), ())), preferred_element_type=F32,
             )
             if q > 0:
                 v = v + acc[sl, :]
             if q < NQ - 1:
                 acc[sl, :] = v
-            elif r:
-                ig_tx[7] = (v * factor).astype(BF)
-                go("IG", 7, ig_tx.at[7], there, sib)
-            else:
-                ig_ref[:, pl.ds(col, BLK)] = (v * factor).astype(BF)
+                continue
+            v = (v * factor).astype(BF)
+            for zz in (0, 1):
+                col = pl.multiple_of(fs_of(at_x(2), zz, c) * BLK, BLK)
+                there = pl.ds(col, BLK)
+                if r:
+                    ig_tx[6 + zz] = v[:, zz * BLK : (zz + 1) * BLK]
+                    go("IG", 6 + zz, ig_tx.at[6 + zz], ig_ref.at[:, there], sib)
+                else:
+                    ig_ref[:, there] = v[:, zz * BLK : (zz + 1) * BLK]
 
     for j in range(NJ):
         got("RRZ", j, rzl.at[chunk(j)])
@@ -391,18 +394,19 @@
     copies = [
         pltpu.make_async_copy(a, b, sem.at[i])
         for i, (a, b) in enumerate(
-            ((ig, ig_out), (ni, ni_out), (nm_v, nm_out), (na_v, na_out), (og_v, og_out))
+            [(nm_v, nm_out), (na_v, na_out), (og_v, og_out), (ni, ni_out)]
+            + [(ig.at[pl.ds(r, 128)], ig_out.at[pl.ds(r, 128)]) for r in range(0, 512, 128)]
         )
     ]
-    copies[0].start()
-    copies[1].start()
+    for cp in copies[3:]:
+        cp.start()
     momentum = 0.9 * mom[...] + delayed[...]
     nm_v[...] = momentum
+    copies[0].start()
+    na_v[...] = anchor[...] - 0.7 * (delayed[...] + 0.9 * momentum)
+    copies[1].start()
+    og_v[...] = anchor[...] - total[...] * 0.125
     copies[2].start()
-    na_v[...] = anchor[...] - 0.7 * (delayed[...] + 0.9 * momentum)
-    copies[3].start()
-    og_v[...] = anchor[...] - total[...] * 0.125
-    copies[4].start()
     for cp in copies:
         cp.wait()
 
@@ -442,7 +446,7 @@
             pltpu.VMEM((PIECE, BLK), F32),
             pltpu.VMEM((PIECE, BLK), F32),
             pltpu.VMEM((PIECE, BLK), F32),
-            pltpu.VMEM((2 * tok, BLK), F32),
+            pltpu.VMEM((2 * tok, 2 * BLK), F32),
             pltpu.SemaphoreType.DMA((N_MSG,)),
             pltpu.SemaphoreType.DMA((N_MSG,)),
             pltpu.SemaphoreType.DMA((6,)),
@@ -457,7 +461,7 @@
         out_shape=(shape((tok, hd), BF), shape(inner_w.shape, BF), f32, f32, f32),
         in_specs=[vm] * 6,
         out_specs=(hbm,) * 5,
-        scratch_shapes=[pltpu.VMEM((PIECE, BLK), F32)] * 3 + [pltpu.SemaphoreType.DMA((5,))],
+        scratch_shapes=[pltpu.VMEM((PIECE, BLK), F32)] * 3 + [pltpu.SemaphoreType.DMA((8,))],
         compiler_params=pltpu.CompilerParams(vmem_limit_bytes=16 * 2**20),
     )(input_grad, new_inner, summed, *across)
     return (input_grad, new_inner, *(v.T for v in rest))

time: 139 us -> 137 us (0.986)
  Pallas kernels: 138 us -> 136 us
where the time goes in v6:
time: 137 us
  Pallas kernels  136 us (99%)
    pallas_call x1, Pallas kernels, per_device(): pl.pallas_call(kernel, out_shape=(pltpu.VMEM((tok, hd), BF), pltpu.VMEM(i...  134 us

profile of v6, /device:TPU:1, one launch (start us, length us, event | category | flops | bytes accessed | tf_op | source)
XLA Modules:
  0.0 137.2 jit_solution(16847492518179853789)
XLA Ops:
  0.6 0.0 copy-start
  0.6 0.0 copy-start.1
  0.7 0.0 copy-start.2
  0.7 134.2 %shard_map.101 = (bf16[512,2048]{1,0:T(8,128)(2,1)S(1)}, bf16[1,128,4608]{2,1,0:T(8,128)(2,1)S(1)}, f32[576,128]{1,0:T(8,128)S(1)}) custom-call(bf16[512,2048]{1,0:T(8,128)(2,1)} %a_hbm.1, bf16[512,4608]{1,0:T(8,128)(2,1)} %g_hbm.1, bf16[1,128,4608]{2,1,0:T(8,128)(2,1)} %w_hbm.1, f32[576,128]{1,0:T(8,128)} %bitcast.6, f32[576,128]{1,0:T(8,128)} %bitcast.8, ...), custom_call_target="tpu_custom_call" | custom-call | tf_op jit(solution)/shard_map/pallas_call | solution.py:421
  134.9 0.0 copy-done
  134.9 0.0 copy-done.1
  134.9 0.0 copy-done.2
  134.9 2.1 %shard_map.102 = (bf16[512,2048]{1,0:T(8,128)(2,1)}, bf16[1,128,4608]{2,1,0:T(8,128)(2,1)}, f32[576,128]{1,0:T(8,128)}, f32[576,128]{1,0:T(8,128)}, f32[576,128]{1,0:T(8,128)}) custom-call(bf16[512,2048]{1,0:T(8,128)(2,1)S(1)} %get-tuple-element.13.ig, bf16[1,128,4608]{2,1,0:T(8,128)(2,1)S(1)} %get-tuple-element.14.ni, ...), custom_call_target="tpu_custom_call" | custom-call | tf_op jit(solution)/shard_map/pallas_call | solution.py:459
Async XLA Ops:
  0.6 134.3 %copy-start = (f32[128,576]{0,1:T(8,128)S(1)}, f32[128,576]{0,1:T(8,128)}, u32[]{:S(2)}) copy-start(f32[128,576]{0,1:T(8,128)} %param.9) | copy-start | bytes 884740
  0.6 134.3 %copy-start.1 = (f32[128,576]{0,1:T(8,128)S(1)}, f32[128,576]{0,1:T(8,128)}, u32[]{:S(2)}) copy-start(f32[128,576]{0,1:T(8,128)} %param.10) | copy-start | bytes 884740
  0.7 134.3 %copy-start.2 = (f32[128,576]{0,1:T(8,128)S(1)}, f32[128,576]{0,1:T(8,128)}, u32[]{:S(2)}) copy-start(f32[128,576]{0,1:T(8,128)} %param.11) | copy-start | bytes 884740

commit v7 on v6

--- a/solution.py
+++ b/solution.py
@@ -18,7 +18,7 @@
 HR = CR // 2
 TILE_N = 1536
 TILE_M = 512
-NQ = 4
+NQ = 6
 PIECE = 576
 WIDE = 640
 

time: 137 us -> 137 us (level)
  no operation moved by 1% of the time
where the time goes in v7:
time: 137 us
  Pallas kernels  136 us (99%)
    pallas_call x1, Pallas kernels, per_device(): pl.pallas_call(kernel, out_shape=(pltpu.VMEM((tok, hd), BF), pltpu.VMEM(i...  134 us

profile of v7, /device:TPU:1, one launch (start us, length us, event | category | flops | bytes accessed | tf_op | source)
XLA Modules:
  0.0 137.2 jit_solution(3192012500620205988)
XLA Ops:
  0.6 0.0 copy-start
  0.6 0.0 copy-start.1
  0.7 0.0 copy-start.2
  0.7 134.2 %shard_map.101 = (bf16[512,2048]{1,0:T(8,128)(2,1)S(1)}, bf16[1,128,4608]{2,1,0:T(8,128)(2,1)S(1)}, f32[576,128]{1,0:T(8,128)S(1)}) custom-call(bf16[512,2048]{1,0:T(8,128)(2,1)} %a_hbm.1, bf16[512,4608]{1,0:T(8,128)(2,1)} %g_hbm.1, bf16[1,128,4608]{2,1,0:T(8,128)(2,1)} %w_hbm.1, f32[576,128]{1,0:T(8,128)} %bitcast.6, f32[576,128]{1,0:T(8,128)} %bitcast.8, ...), custom_call_target="tpu_custom_call" | custom-call | tf_op jit(solution)/shard_map/pallas_call | solution.py:421
  134.9 0.0 copy-done
  134.9 0.0 copy-done.1
  134.9 0.0 copy-done.2
  134.9 2.1 %shard_map.102 = (bf16[512,2048]{1,0:T(8,128)(2,1)}, bf16[1,128,4608]{2,1,0:T(8,128)(2,1)}, f32[576,128]{1,0:T(8,128)}, f32[576,128]{1,0:T(8,128)}, f32[576,128]{1,0:T(8,128)}) custom-call(bf16[512,2048]{1,0:T(8,128)(2,1)S(1)} %get-tuple-element.13.ig, bf16[1,128,4608]{2,1,0:T(8,128)(2,1)S(1)} %get-tuple-element.14.ni, ...), custom_call_target="tpu_custom_call" | custom-call | tf_op jit(solution)/shard_map/pallas_call | solution.py:459
Async XLA Ops:
  0.6 134.2 %copy-start = (f32[128,576]{0,1:T(8,128)S(1)}, f32[128,576]{0,1:T(8,128)}, u32[]{:S(2)}) copy-start(f32[128,576]{0,1:T(8,128)} %param.9) | copy-start | bytes 884740
  0.6 134.2 %copy-start.1 = (f32[128,576]{0,1:T(8,128)S(1)}, f32[128,576]{0,1:T(8,128)}, u32[]{:S(2)}) copy-start(f32[128,576]{0,1:T(8,128)} %param.10) | copy-start | bytes 884740
  0.7 134.2 %copy-start.2 = (f32[128,576]{0,1:T(8,128)S(1)}, f32[128,576]{0,1:T(8,128)}, u32[]{:S(2)}) copy-start(f32[128,576]{0,1:T(8,128)} %param.11) | copy-start | bytes 884740
